TPU v7x, 32 devices: a whole 2x2x4 slice. The times are simulated.
32 devices in a mesh: grp: 2 (over x), chan: 16 (over z, y, core).
Axes of the slice: x: 2, y: 2, z: 4, core: 2. Of those that a mesh axis runs over, the one named last changes fastest.
Arguments:
- voltages: bfloat16 [2, 2048, 12032], P(None, ('grp', 'chan')), parts along dimension 1, may hold values from -6 to 6
- fir_taps: bfloat16 [16, 256], replicated, may hold values from -1.5 to 1.5
- positions: float32 [2, 512], replicated, may hold values from -40 to 40
- cal_amp: float32 [512, 16], P('grp'), parts along dimension 0, may hold values from 0.5 to 2
- cal_phase: float32 [512, 16], P('grp'), parts along dimension 0, may hold values from -3.140625 to 3.140625
- cal_index: int32 [1024], replicated, may hold values from 0 to 255
- owner_counts: int32 [32], P('grp'), parts along dimension 0, may hold values from 0 to 32, as said below
- tile_owner: int32 [32], P('grp'), parts along dimension 0, may hold values from 0 to 15, each once
Outputs:
- owner_images: float32 [32, 16, 256], P(('grp', 'chan')), parts along dimension 0
- subband_autos: float32 [32, 1024], P(('grp', 'chan')), parts along dimension 0
There are 2 independent parts, one for each index of `grp`. A program takes and returns all parts, laid end to end along the dimension named above; an argument that names none is the same for every part. Nothing has to cross between parts.
Inputs may be any that keep to these rules, and one draw needn't show every extreme that they name: `owner_counts`: the counts sum to 256; one subband holds exactly 32 channels and one holds none. `tile_owner`: A permutation of the tiles.
All inputs are finite; a program needn't handle non-finite values.
Results may differ from a plain program's by a relative error of at most 0.0064.
Values may be sent and summed in bfloat16 or wider, within the bound.
A program may use at most 192 MiB of HBM per device.

v0:
```python
import math

import jax
import jax.numpy as jnp
from jax import lax
from jax.sharding import PartitionSpec as P

NIN = 1024
CH = 256
AVG = 16
GROUPS = 16
SB = 16
BLOCKS = 2
SPEC = 32
SIDE = 64
PIX = 4096
NCAL = 256


highest = lax.Precision.HIGHEST


def dft_table(length):
    indices = jnp.arange(length, dtype=jnp.int32)
    products = indices[:, None] * indices[None, :] % length
    angles = products.astype(jnp.float32) * jnp.float32(2.0 * math.pi / length)
    scaling = jnp.float32(1.0 / math.sqrt(length))
    cosine = jnp.cos(angles) * scaling
    sine_part = jnp.sin(angles) * scaling
    upper_half = jnp.stack([cosine, sine_part], axis=1)
    lower_half = jnp.stack([-sine_part, cosine], axis=1)
    return jnp.stack([upper_half, lower_half], axis=1).astype(jnp.bfloat16)


def steering_table(positions, side):
    pixel_ids = jnp.arange(side * side, dtype=jnp.int32)
    centre = side // 2
    across = (pixel_ids // side - centre).astype(jnp.float32) / jnp.float32(side)
    upward = (pixel_ids % side - centre).astype(jnp.float32) / jnp.float32(side)
    east_pos = jnp.repeat(positions[0], 2)
    north_pos = jnp.repeat(positions[1], 2)
    phases = jnp.float32(2.0 * math.pi) * (
        east_pos[:, None] * across[None, :] + north_pos[:, None] * upward[None, :]
    )
    return jnp.stack([jnp.cos(phases), -jnp.sin(phases)])


def filter_block(voltage, fir_taps, first_spectrum, spectra_count):
    taps_total = fir_taps.shape[0]
    length = fir_taps.shape[1]
    span_len = (spectra_count + taps_total - 1) * length
    window = voltage[:, :, first_spectrum * length : first_spectrum * length + span_len]
    window = window.reshape(
        voltage.shape[0], voltage.shape[1], spectra_count + taps_total - 1, length
    )
    summed = jnp.zeros((voltage.shape[0], voltage.shape[1], spectra_count, length), jnp.float32)
    for tap_index in range(taps_total):
        summed = summed + window[:, :, tap_index : tap_index + spectra_count, :].astype(
            jnp.float32
        ) * fir_taps[tap_index].astype(jnp.float32)
    return summed.astype(jnp.bfloat16)


def local(voltages, fir_taps, positions, cal_amp, cal_phase, cal_index, owner_counts, tile_owner):
    devices = lax.axis_size("chan")
    myself = lax.axis_index("chan")
    in_dev = voltages.shape[1]
    input_total = in_dev * devices
    chan_dev = CH // devices
    dft_rows = dft_table(CH)
    offsets = jnp.cumsum(owner_counts) - owner_counts
    device_ids = jnp.arange(devices, dtype=jnp.int32)
    capacity = 2 * chan_dev
    slot_total = (capacity + AVG - 2) // AVG + 1
    slot_ids = jnp.arange(capacity, dtype=jnp.int32)
    wanted = jnp.minimum(offsets[:, None] + slot_ids[None, :], CH - 1)
    present = slot_ids[None, :] < owner_counts[:, None]
    received = []
    for block_index in range(BLOCKS):
        filtered = filter_block(voltages, fir_taps, block_index * SB, SB)
        spectra = jnp.einsum(
            "qrk,cpqk->cpr",
            filtered.reshape(2, in_dev * SB, CH),
            dft_rows,
            preferred_element_type=jnp.float32,
        ).astype(jnp.bfloat16)
        outgoing = jnp.where(
            present[:, :, None, None], spectra[wanted], jnp.zeros((), jnp.bfloat16)
        )
        received.append(lax.all_to_all(outgoing, "chan", split_axis=0, concat_axis=0, tiled=True))
    stacked = jnp.stack(received).reshape(BLOCKS, devices, capacity, 2, in_dev, SB)
    cal_ids = jnp.arange(NCAL, dtype=jnp.int32)
    selection = (cal_index[:, None] == cal_ids[None, :]).astype(jnp.float32)
    real_gain = jnp.dot(selection, cal_amp * jnp.cos(cal_phase), precision=highest).T
    imag_gain = jnp.dot(selection, cal_amp * jnp.sin(cal_phase), precision=highest).T
    steering = steering_table(positions, SIDE)
    steer_flat = steering.reshape(2 * input_total, PIX)
    image_scale = jnp.float32(math.sqrt(SPEC * AVG) / NIN)
    my_count = owner_counts[myself]
    my_offset = offsets[myself]
    first_group = my_offset // AVG
    spectra_inverse = jnp.float32(1.0 / (SPEC * AVG))
    contract = (((1,), (1,)), ((), ()))

    def correlate(slot_index, carry):
        partial_value, auto_rows = carry
        picked = lax.dynamic_index_in_dim(stacked, slot_index, 2, keepdims=False)
        inputs_rows = jnp.transpose(picked, (2, 1, 3, 0, 4)).reshape(2, input_total, SPEC)
        joined = jnp.concatenate([inputs_rows[0], inputs_rows[1]], axis=1)
        is_live = slot_index < my_count
        weight = jnp.where(is_live, spectra_inverse, jnp.float32(0.0))
        turned = jnp.concatenate([inputs_rows[1], -inputs_rows[0]], axis=1)
        vis_real = lax.dot_general(joined, joined, contract, preferred_element_type=jnp.float32)
        vis_imag = lax.dot_general(turned, joined, contract, preferred_element_type=jnp.float32)
        group_slot = jnp.clip((my_offset + slot_index) // AVG - first_group, 0, slot_total - 1)
        current = lax.dynamic_index_in_dim(partial_value, group_slot, 0, keepdims=False)
        updated = current + weight * jnp.stack([vis_real, vis_imag])
        partial_value = lax.dynamic_update_index_in_dim(partial_value, updated, group_slot, 0)
        joined_float = joined.astype(jnp.float32)
        power_sum = jnp.sum(joined_float * joined_float, axis=1) / jnp.float32(SPEC)
        power_sum = jnp.where(is_live, power_sum, jnp.float32(0.0))
        auto_rows = lax.dynamic_update_index_in_dim(auto_rows, power_sum, slot_index, 0)
        return (partial_value, auto_rows)

    start_autos = jnp.zeros((capacity, input_total), jnp.float32)
    start_partial = jnp.zeros((slot_total, 2, input_total, input_total), jnp.float32)
    partial_value, auto_rows = lax.fori_loop(0, capacity, correlate, (start_partial, start_autos))
    outgoing_rows = partial_value.reshape(slot_total, 2, devices, in_dev * input_total)
    incoming = lax.all_to_all(outgoing_rows, "chan", split_axis=2, concat_axis=2, tiled=True)
    sender_first = offsets // AVG
    sender_last = (offsets + owner_counts - 1) // AVG
    group_of = sender_first[None, :] + jnp.arange(slot_total, dtype=jnp.int32)[:, None]
    slot_used = (owner_counts[None, :] > 0) & (group_of <= sender_last[None, :])
    group_ids = jnp.arange(GROUPS, dtype=jnp.int32)
    selector = ((group_of[:, :, None] == group_ids[None, None, :]) & slot_used[:, :, None]).astype(
        jnp.float32
    )
    averaged = jnp.einsum("tsg,tpsx->gpx", selector, incoming, precision=highest).reshape(
        GROUPS, 2, in_dev, input_total
    )
    row_start = myself * in_dev
    row_real = lax.dynamic_slice_in_dim(real_gain, row_start, in_dev, 1)
    row_imag = lax.dynamic_slice_in_dim(imag_gain, row_start, in_dev, 1)
    pair_real = (
        row_real[:, :, None] * real_gain[:, None, :] + row_imag[:, :, None] * imag_gain[:, None, :]
    )
    pair_imag = (
        row_imag[:, :, None] * real_gain[:, None, :] - row_real[:, :, None] * imag_gain[:, None, :]
    )
    vis_real = averaged[:, 0]
    vis_imag = averaged[:, 1]
    row_ids = row_start + jnp.arange(in_dev, dtype=jnp.int32)
    on_diagonal = row_ids[:, None] == jnp.arange(input_total, dtype=jnp.int32)[None, :]
    cal_real = jnp.where(on_diagonal, jnp.float32(0.0), pair_real * vis_real - pair_imag * vis_imag)
    cal_imag = jnp.where(on_diagonal, jnp.float32(0.0), pair_real * vis_imag + pair_imag * vis_real)
    upper_rows = jnp.concatenate([cal_real, -cal_imag], axis=2)
    lower_rows = jnp.concatenate([cal_imag, cal_real], axis=2)
    left_rows = jnp.stack([upper_rows, lower_rows], axis=1).reshape(
        GROUPS * 2 * in_dev, 2 * input_total
    )
    beam_sums = jnp.dot(
        left_rows, steer_flat, precision=highest, preferred_element_type=jnp.float32
    )
    beam_sums = beam_sums.reshape(GROUPS, 2, in_dev, PIX)
    own_steer = lax.dynamic_slice_in_dim(steering, row_start, in_dev, 1)
    partial_image = image_scale * jnp.sum(
        own_steer[0][None] * beam_sums[:, 0] + own_steer[1][None] * beam_sums[:, 1], axis=1
    )
    tile_pix = PIX // devices
    summed_image = lax.psum(partial_image, "chan")
    my_tile = jnp.sum(jnp.where(tile_owner == myself, device_ids, 0))
    my_piece = lax.dynamic_slice_in_dim(summed_image, my_tile * tile_pix, tile_pix, 1)
    result = my_piece[None]
    my_size = owner_counts[myself]
    divisor = jnp.maximum(my_size, 1).astype(jnp.float32)
    sub_autos = jnp.sum(auto_rows, axis=0) / divisor
    return (result, sub_autos[None, :])


def solution(mesh):
    in_specs = (
        P(None, ("grp", "chan"), None),
        P(),
        P(),
        P("grp", None),
        P("grp", None),
        P(),
        P("grp"),
        P("grp"),
    )
    out_specs = (P(("grp", "chan"), None, None), P(("grp", "chan"), None))
    return jax.shard_map(local, mesh=mesh, in_specs=in_specs, out_specs=out_specs, check_vma=False)
```

profile of v0, /device:TPU:0, one launch (start us, length us, event | category | flops | bytes accessed | tf_op | source)
XLA Modules:
  0.0 1563.6 jit_solution(14423600311540269187)
XLA Ops:
  36.7 16.7 %gather_fusion = bf16[512,2,1024]{2,1,0:T(2,128)(2,1)} fusion(bf16[256,2,1024]{2,1,0:T(2,128)(2,1)S(1)} %copy.47, s32[1024]{0:T(1024)S(1)} %pad_clamp_fusion), kind=kCustom, calls=%fused_computation | custom fusion | bytes 4196352 | tf_op jit(solution)/shard_map/gather | solution.py:88
  53.4 17.0 %gather_fusion.1 = bf16[512,2,1024]{2,1,0:T(2,128)(2,1)} fusion(bf16[256,2,1024]{2,1,0:T(2,128)(2,1)S(1)} %copy.50, s32[1024]{0:T(1024)S(1)} %pad_clamp_fusion), kind=kCustom, calls=%fused_computation.1 | custom fusion | bytes 4196352 | tf_op jit(solution)/shard_map/gather | solution.py:88
  74.2 54.6 %all_to_all.15 = bf16[16,32,2,1024]{3,1,2,0:T(8,128)(2,1)} all-to-all(bf16[16,32,2,1024]{3,1,2,0:T(8,128)(2,1)S(1)} %get-tuple-element.262), channel_id=1, replica_groups=mesh['grp'=2,'chan'=16] {'chan'}, dimensions={0} | all-to-all | bytes 4194304 | tf_op jit(solution)/shard_map/all_to_all | solution.py:90
  137.4 7.8 copy.52
  145.2 29.9 %all-to-all-done = bf16[16,32,2,1024]{3,1,2,0:T(8,128)(2,1)S(1)} async-done(((bf16[16,32,2,1024]{3,1,2,0:T(8,128)(2,1)}), bf16[16,32,2,1024]{3,1,2,0:T(8,128)(2,1)S(1)}, u32[]{:S(2)}, u32[]{:S(2)}) %all-to-all-start) | async-done | bytes 2097184 | tf_op jit(solution)/shard_map/all_to_all | solution.py:90
  181.0 14.7 pad_maximum_fusion.1
  195.7 22.5 %copy.53 = bf16[2,16,32,2,64,16]{4,1,5,0,3,2:T(8,128)(2,1)} copy(bf16[2,16,32,2,64,16]{2,5,4,3,1,0:T(8,128)(2,1)} %pad_maximum_fusion.1) | data formatting | bytes 8388608 | tf_op jit(solution)/shard_map/while | solution.py:127
  218.2 11.5 broadcast_in_dim.50
  229.7 338.3 %while.17 = (s32[]{:T(128)}, f32[3,2,1024,1024]{3,2,1,0:T(8,128)}, f32[32,1024]{1,0:T(8,128)S(1)}, s32[]{:T(128)}, s32[]{:T(128)}, /*index=5*/s32[]{:T(128)}, bf...) while((s32[]{:T(128)}, f32[3,2,1024,1024]{3,2,1,0:T(8,128)}, ...), condition=%wide.region_3.4_spmd, body=%wide.region_1.3_spmd.sunk | while | flops 275284992 | bytes 35213696 | solution.py:127
  402.9 6.4 fusion.82
  445.2 6.4 fusion.82
  455.8 6.4 fusion.82
  466.4 6.4 fusion.82
  519.3 6.4 fusion.82
  568.1 21.6 %reshape.724 = f32[3,2,16,65536]{3,2,1,0:T(8,128)} reshape(f32[3,2,1024,1024]{3,2,1,0:T(8,128)} %get-tuple-element.180) | data formatting | bytes 50331648 | tf_op jit(solution)/shard_map/reshape | solution.py:128
  589.7 41.9 %copy.54 = f32[3,2,16,65536]{3,1,0,2:T(2,128)} copy(f32[3,2,16,65536]{3,2,1,0:T(8,128)} %reshape.724) | data formatting | bytes 50331648 | tf_op jit(solution)/shard_map/reshape | solution.py:128
  631.6 11.5 all-to-all-start.2
  646.7 62.5 %fusion.16 = (f32[1,1024,4096]{2,1,0:T(8,128)S(1)}, f32[1,1024,4096]{2,1,0:T(8,128)S(1)}) fusion(f32[4096]{0:T(1024)S(1)} %get-tuple-element.265, f32[1024]{0:T(1024)S(1)} %mul.524, f32[4096]{0:T(1024)S(1)} %get-tuple-element.264, f32[1024]{0:T(1024)S(1)} %mul.520), kind=kLoop, calls=%fused_computation.34 | loop fusion | flops 20971520 | bytes 33595392 | tf_op jit(solution)/shard_map/cos | solution.py:45
  710.6 11.2 pad_maximum_fusion
  721.8 364.1 %all-to-all-done.2 = f32[3,2,16,65536]{3,1,0,2:T(2,128)} async-done(((f32[3,2,16,65536]{3,1,0,2:T(2,128)}), f32[3,2,16,65536]{3,1,0,2:T(2,128)}, u32[]{:S(2)}, u32[]{:S(2)}) %all-to-all-start.2) | async-done | bytes 25165856 | tf_op jit(solution)/shard_map/all_to_all | solution.py:129
  1085.9 28.2 %fusion.6 = f32[16,2,65536,1]{2,0,3,1:T(8,128)S(1)} fusion(f32[3,2,16,65536]{3,1,0,2:T(2,128)} %all-to-all-done.2, s32[3,16]{1,0:T(4,128)S(1)} %iota_add_fusion, pred[3,16]{1,0:T(4,128)(4,1)S(1)} %compare_and_fusion), kind=kOutput, calls=%fused_computation.19 | convolution fusion | flops 1207961088 | bytes 33554672 | tf_op jit(solution)/shard_map/tsg,tpsx->gpx/dot_general | solution.py:138
  1128.1 226.1 %fusion.12 = f32[16,2,64,4096]{3,2,1,0:T(8,128)} fusion(f32[2048,4096,1,1]{1,0,3,2:T(8,128)} %bitcast.143, f32[16,1,64,2048]{3,2,1,0:T(8,128)} %get-tuple-element.234, f32[16,1,64,2048]{3,2,1,0:T(8,128)} %get-tuple-element.233), kind=kOutput, calls=%fused_computation.28 | convolution fusion | flops 206162624512 | bytes 83886080 | tf_op jit(solution)/shard_map/dot_general | solution.py:161
  1354.2 12.2 fusion.10
  1367.8 187.5 %all-reduce.2.cloned.1.call-done = f32[16,4096]{1,0:T(8,128)} async-done(((f32[16,4096]{1,0:T(8,128)}), f32[16,4096]{1,0:T(8,128)}) %all-reduce.2.cloned.1.call-update) | async-done | bytes 262160 | tf_op jit(solution)/shard_map/psum | solution.py:170
  (449 shorter events, 331.8 us)
Async XLA Ops:
  21.0 4.4 copy-start.2
  30.4 4.4 copy-start.3
  53.4 17.0 %copy-start = (bf16[512,2,1024]{2,1,0:T(2,128)(2,1)S(1)}, bf16[512,2,1024]{2,1,0:T(2,128)(2,1)}, u32[]{:S(2)}) copy-start(bf16[512,2,1024]{2,1,0:T(2,128)(2,1)} %gather_fusion) | copy-start | bytes 6291460
  128.8 5.3 copy-start.4
  128.8 46.4 %all-to-all-start = ((bf16[16,32,2,1024]{3,1,2,0:T(8,128)(2,1)}), bf16[16,32,2,1024]{3,1,2,0:T(8,128)(2,1)S(1)}, u32[]{:S(2)}, u32[]{:S(2)}) async-start(bf16[16,32,2,1024]{3,1,2,0:T(8,128)(2,1)} %get-tuple-element.261), calls=%async_computation | async-start | bytes 4194304 | tf_op jit(solution)/shard_map/all_to_all | solution.py:90
  631.5 12.8 copy-start.5
  631.5 13.5 copy-start.6
  631.6 13.5 copy-start.7
  631.6 13.5 copy-start.8
  631.6 454.3 %all-to-all-start.2 = ((f32[3,2,16,65536]{3,1,0,2:T(2,128)}), f32[3,2,16,65536]{3,1,0,2:T(2,128)}, u32[]{:S(2)}, u32[]{:S(2)}) async-start(f32[3,2,16,65536]{3,1,0,2:T(2,128)} %copy.54), calls=%async_computation.2 | async-start | bytes 50331648 | tf_op jit(solution)/shard_map/all_to_all | solution.py:129
  643.1 912.2 %all-reduce.2.cloned.1.call-start = ((), (), s32[]{:S(2)}) async-start(), calls=%async_computation.3 | async-start | bytes 524288 | tf_op jit(solution)/shard_map/psum | solution.py:170
  1128.1 226.1 %copy-start.1 = (f32[64,4096]{1,0:T(8,128)S(1)}, f32[64,4096]{1,0:T(8,128)}, u32[]{:S(2)}) copy-start(f32[64,4096]{1,0:T(8,128)} %get-tuple-element.238) | copy-start | bytes 3145732
Sparse Core Ops, SparseCore 0:
  1367.3 187.9 all-reduce.1
where the time goes:
time: 1570 us; the launch traced here: 1560 us
  waiting for transfers between devices  582 us (37%)
  other arithmetic  336 us (21%)
  matrix products  304 us (19%)
  local copies, waits for them, and re-layouts  212 us (14%)
  blocking collectives  54.6 us (3%)
  loops' own time  40.2 us (3%)
  between operations  18.1 us (1%)
  starting transfers between devices  16.8 us (1%)
    all_to_all x1, waiting for transfers between devices, local(): lax.all_to_all(outgoing_rows, 'chan', split_axis=2, concat_axis=2, tiled=...  364 us
    dot_general x1, matrix products, local(): jnp.dot(left_rows, steer_flat, precision=highest, preferred_element_type=...  226 us
    dynamic_update_slice x32, other arithmetic, correlate(): lax.dynamic_update_index_in_dim(partial_value, updated, group_slot, 0)  205 us
    psum x1, waiting for transfers between devices, local(): summed_image = lax.psum(partial_image, 'chan')  188 us
    reshape x2, local copies, waits for them, and re-layouts, local(): partial_value.reshape(slot_total, 2, devices, in_dev * input_total)  63.5 us
    cos x1, other arithmetic, steering_table(): return jnp.stack([jnp.cos(phases), -jnp.sin(phases)])  62.5 us
    all_to_all x1, blocking collectives, local(): lax.all_to_all(outgoing, 'chan', split_axis=0, concat_axis=0, tiled=True)  54.6 us
    another operation x1, loops' own time, local(): lax.fori_loop(0, capacity, correlate, (start_partial, start_autos))  40.2 us
  transfers between devices with their start and end apart: 3, of which 3 were waited for; matrix products, arithmetic and copies ran while one was open for 6% of the time, Pallas kernels for 0%

commit v1 on v0

v1 whole, which is shorter than its diff:
```python
import math

import jax
import jax.numpy as jnp
from jax import lax
from jax.sharding import PartitionSpec as P

CH = 256
AVG = 16
GROUPS = 16
SPEC = 32
TAPS = 16
SIDE = 64
PIX = 4096
NCAL = 256

highest = lax.Precision.HIGHEST


def dft_table(length):
    indices = jnp.arange(length, dtype=jnp.int32)
    products = indices[:, None] * indices[None, :] % length
    angles = products.astype(jnp.float32) * jnp.float32(2.0 * math.pi / length)
    scaling = jnp.float32(1.0 / math.sqrt(length))
    cosine = jnp.cos(angles) * scaling
    sine_part = jnp.sin(angles) * scaling
    upper_half = jnp.stack([cosine, sine_part], axis=1)
    lower_half = jnp.stack([-sine_part, cosine], axis=1)
    return jnp.stack([upper_half, lower_half], axis=1).astype(jnp.bfloat16)


def steering_tables(positions):
    steps = (jnp.arange(SIDE, dtype=jnp.float32) - SIDE // 2) / jnp.float32(SIDE)
    turn = jnp.float32(2.0 * math.pi)
    east = turn * (steps[:, None] * positions[0][None, :])
    north = turn * (steps[:, None] * positions[1][None, :])
    east_cos, east_sin = lax.optimization_barrier((jnp.cos(east), jnp.sin(east)))
    north_cos, north_sin = lax.optimization_barrier((jnp.cos(north), jnp.sin(north)))
    cosine = east_cos[:, None] * north_cos[None] - east_sin[:, None] * north_sin[None]
    sine = east_sin[:, None] * north_cos[None] + east_cos[:, None] * north_sin[None]
    stations = positions.shape[1]
    return (
        cosine.reshape(PIX, stations).astype(jnp.bfloat16),
        sine.reshape(PIX, stations).astype(jnp.bfloat16),
    )


def polyphase(voltage, fir_taps):
    length = fir_taps.shape[1]
    window = voltage.reshape(voltage.shape[0], voltage.shape[1], -1, length)
    summed = jnp.zeros((voltage.shape[0], voltage.shape[1], SPEC, length), jnp.float32)
    for tap_index in range(TAPS):
        summed = summed + window[:, :, tap_index : tap_index + SPEC, :].astype(
            jnp.float32
        ) * fir_taps[tap_index].astype(jnp.float32)
    return summed.astype(jnp.bfloat16)


def local(voltages, fir_taps, positions, cal_amp, cal_phase, cal_index, owner_counts, tile_owner):
    devices = lax.axis_size("chan")
    myself = lax.axis_index("chan")
    in_dev = voltages.shape[1]
    st_dev = in_dev // 2
    stations = st_dev * devices
    chan_dev = CH // devices
    per_group = AVG // chan_dev

    my_index = lax.dynamic_slice_in_dim(cal_index, myself * in_dev, in_dev, 0)
    selection = (my_index[:, None] == jnp.arange(NCAL, dtype=jnp.int32)[None, :]).astype(jnp.float32)
    gain_re = jnp.dot(selection, cal_amp * jnp.cos(cal_phase), precision=highest).T
    gain_im = jnp.dot(selection, cal_amp * jnp.sin(cal_phase), precision=highest).T

    filtered = polyphase(voltages, fir_taps)
    spectra = jnp.einsum(
        "qrk,cpqk->cpr",
        filtered.reshape(2, in_dev * SPEC, CH),
        dft_table(CH),
        preferred_element_type=jnp.float32,
    ).astype(jnp.bfloat16)
    values = spectra.astype(jnp.float32).reshape(GROUPS, AVG, 2, st_dev, 2, SPEC)

    powers = jnp.sum(values * values, axis=(2, 5))
    power_rows = powers.reshape(CH, in_dev) / jnp.float32(SPEC)
    offsets = jnp.cumsum(owner_counts) - owner_counts
    chan_ids = jnp.arange(CH, dtype=jnp.int32)
    member = (
        (chan_ids[None, :] >= offsets[:, None])
        & (chan_ids[None, :] < (offsets + owner_counts)[:, None])
    ).astype(jnp.float32)
    divisor = jnp.maximum(owner_counts, 1).astype(jnp.float32)
    sub_rows = jnp.dot(member, power_rows, precision=highest) / divisor[:, None]

    gre = gain_re.reshape(GROUPS, 1, st_dev, 2, 1)
    gim = gain_im.reshape(GROUPS, 1, st_dev, 2, 1)
    cal_re = values[:, :, 0] * gre - values[:, :, 1] * gim
    cal_im = values[:, :, 0] * gim + values[:, :, 1] * gre
    sum_re = cal_re[:, :, :, 0] + cal_re[:, :, :, 1]
    sum_im = cal_im[:, :, :, 0] + cal_im[:, :, :, 1]
    crossed = 2.0 * (
        cal_re[:, :, :, 0] * cal_re[:, :, :, 1] + cal_im[:, :, :, 0] * cal_im[:, :, :, 1]
    )
    cross_power = jnp.sum(crossed, axis=(1, 2, 3))
    outgoing = jnp.stack([sum_re, sum_im], axis=0).astype(jnp.bfloat16)
    outgoing = outgoing.reshape(2, devices, chan_dev, st_dev, SPEC)
    outgoing = jnp.transpose(outgoing, (1, 0, 3, 2, 4)).reshape(
        devices, 2, st_dev, chan_dev * SPEC
    )
    incoming = lax.all_to_all(outgoing, "chan", split_axis=0, concat_axis=0, tiled=True)

    cosine, sine = steering_tables(positions)
    joined = jnp.transpose(incoming, (1, 0, 2, 3)).reshape(2, stations, chan_dev * SPEC)
    real, imag = joined[0], joined[1]
    contract = (((1,), (1,)), ((), ()))
    along = jnp.concatenate([real, imag], axis=1)
    turned = jnp.concatenate([imag, -real], axis=1)
    even = lax.dot_general(along, along, contract, preferred_element_type=jnp.float32)
    odd = lax.dot_general(turned, along, contract, preferred_element_type=jnp.float32)
    station_ids = jnp.arange(stations, dtype=jnp.int32)
    on_diagonal = station_ids[:, None] == station_ids[None, :]
    even = jnp.where(on_diagonal, jnp.float32(0.0), even).astype(jnp.bfloat16)
    odd = jnp.where(on_diagonal, jnp.float32(0.0), -2.0 * odd).astype(jnp.bfloat16)
    first = jnp.dot(cosine, even, preferred_element_type=jnp.float32) + jnp.dot(
        sine, odd, preferred_element_type=jnp.float32
    )
    second = jnp.dot(sine, even, preferred_element_type=jnp.float32)
    image = jnp.sum(
        cosine.astype(jnp.float32) * first + sine.astype(jnp.float32) * second, axis=1
    )

    tile_pix = PIX // devices
    device_ids = jnp.arange(devices, dtype=jnp.int32)
    tile_of = jnp.sum(
        jnp.where(tile_owner[None, :] == device_ids[:, None], device_ids[None, :], 0), axis=1
    )
    tiles = image.reshape(devices, tile_pix)[tile_of]
    last = jnp.concatenate(
        [tiles, sub_rows, jnp.broadcast_to(cross_power[None], (devices, GROUPS))], axis=1
    )
    arrived = lax.all_to_all(last, "chan", split_axis=0, concat_axis=0, tiled=True)
    scale = jnp.float32(1.0 / (SPEC * AVG) * math.sqrt(SPEC * AVG) / (2 * stations))
    pieces = jnp.sum(arrived[:, :tile_pix].reshape(GROUPS, per_group, tile_pix), axis=1)
    constant = jnp.sum(arrived[:, tile_pix + in_dev :], axis=0)
    result = scale * (pieces + constant[:, None])
    autos = arrived[:, tile_pix : tile_pix + in_dev].reshape(1, devices * in_dev)
    return (result[None], autos)


def solution(mesh):
    in_specs = (
        P(None, ("grp", "chan"), None),
        P(),
        P(),
        P("grp", None),
        P("grp", None),
        P(),
        P("grp"),
        P("grp"),
    )
    out_specs = (P(("grp", "chan"), None, None), P(("grp", "chan"), None))
    return jax.shard_map(local, mesh=mesh, in_specs=in_specs, out_specs=out_specs, check_vma=False)
```

time: 1570 us -> 177 us (0.11)
  waiting for transfers between devices: 582 us -> 0.02 us
  other arithmetic: 336 us -> 46.9 us
  matrix products: 304 us -> 33.9 us
  local copies, waits for them, and re-layouts: 212 us -> 75 us
  blocking collectives: 54.6 us -> 12.4 us
  loops' own time: 40.2 us -> 0 us
  between operations: 18.1 us -> 0.85 us
    all_to_all x1 -> x0, waiting for transfers between devices: 364 us -> none  [local(): lax.all_to_all(outgoing_rows, 'chan', split_axis=2, concat_axis=2, tiled=...]
    dot_general x68 -> x6, matrix products: 302 us -> 30.7 us  [the longest x1 10.1 us: local(): second = jnp.dot(sine, even, preferred_element_type=jnp.float32)]
    dynamic_update_slice x32 -> x0, other arithmetic: 205 us -> none  [correlate(): lax.dynamic_update_index_in_dim(partial_value, updated, group_slot, 0)]
    psum x1 -> x0, waiting for transfers between devices: 188 us -> none  [local(): summed_image = lax.psum(partial_image, 'chan')]
    cos x1 -> x0, other arithmetic: 62.5 us -> none  [steering_table(): return jnp.stack([jnp.cos(phases), -jnp.sin(phases)])]
    all_to_all x1, blocking collectives: 54.6 us -> 12.4 us  [local(): lax.all_to_all(last, 'chan', split_axis=0, concat_axis=0, tiled=True)]
    another operation x1 -> x0, loops' own time: 40.2 us -> none  [local(): lax.fori_loop(0, capacity, correlate, (start_partial, start_autos))]
    reshape x4 -> x5, local copies, waits for them, and re-layouts: 69.7 us -> 29.9 us  [the longest x1 18 us: local(): spectra.astype(jnp.float32).reshape(GROUPS, AVG, 2, st_dev, 2, SPEC)]
  transfers between devices with their start and end apart: 3 -> 1, of which waited for: 3 -> 0; matrix products, arithmetic and copies ran while one was open for 6% -> 26% of each run, Pallas kernels for 0% -> 0%
where the time goes in v1:
time: 177 us; the launch traced here: 176 us
  local copies, waits for them, and re-layouts  75 us (42%)
  other arithmetic  46.9 us (26%)
  matrix products  33.9 us (19%)
  blocking collectives  12.4 us (7%)
  starting transfers between devices  7.38 us (4%)
    reshape x1, local copies, waits for them, and re-layouts, local(): spectra.astype(jnp.float32).reshape(GROUPS, AVG, 2, st_dev, 2, SPEC)  18 us
    slice x1, local copies, waits for them, and re-layouts, local(): cal_re = values[:, :, 0] * gre - values[:, :, 1] * gim  13.9 us
    reduce_sum x1, other arithmetic, local(): powers = jnp.sum(values * values, axis=(2, 5))  13 us
    all_to_all x1, blocking collectives, local(): lax.all_to_all(last, 'chan', split_axis=0, concat_axis=0, tiled=True)  12.4 us
    reduce_sum x2, local copies, waits for them, and re-layouts, local(): powers = jnp.sum(values * values, axis=(2, 5))  11.9 us
    dot_general x1, matrix products, local(): second = jnp.dot(sine, even, preferred_element_type=jnp.float32)  10.1 us
    convert_element_type x1, other arithmetic, polyphase(): return summed.astype(jnp.bfloat16)  9.7 us
    dot_general x1, matrix products, local(): jnp.dot(sine, odd, preferred_element_type=jnp.float32)  8.41 us
  transfers between devices with their start and end apart: 1, of which 0 were waited for; matrix products, arithmetic and copies ran while one was open for 26% of the time, Pallas kernels for 0%

profile of v1, /device:TPU:0, one launch (start us, length us, event | category | flops | bytes accessed | tf_op | source)
XLA Modules:
  0.0 176.3 jit_solution(14124087088271739654)
XLA Ops:
  0.6 1.1 negate_convert_fusion
  3.5 1.6 fusion.29
  5.1 1.6 fusion.28
  6.6 1.7 slice_convert_fusion.15
  8.3 4.4 %reshape.352 = bf16[2,64,47,256]{3,2,1,0:T(8,128)(2,1)S(1)} reshape(bf16[2,64,12032]{2,1,0:T(8,128)(2,1)} %param.8) | data formatting | bytes 6160384 | tf_op jit(solution)/shard_map/reshape | solution.py:50
  12.8 9.7 %add_convert_fusion.3 = bf16[2,64,32,256]{3,2,1,0:T(8,128)(2,1)S(1)} fusion(bf16[2,64,47,256]{3,2,1,0:T(8,128)(2,1)S(1)} %reshape.352, f32[256]{0:T(256)} %bitcast.115, f32[256]{0:T(256)} %bitcast.116, f32[256]{0:T(256)S(1)} %bitcast.102, f32[256]{0:T(256)S(1)} %bitcast.103, f32[256]{0:T(256)S(1)} %bitcast.104, f32[256]{0:T(256)} %bitcast.105, ...), kind=kLoop, calls=%fused_computation.14 | loop fusion | flops 50331648 | bytes 35667968 | tf_op jit(solution)/shard_map/convert_element_type | solution.py:56
  22.5 3.4 %multiply_reduce_fusion.1 = (f32[256,2048]{1,0:T(8,128)S(1)}, f32[256,2,2048]{2,0,1:T(8,128)}) fusion(bf16[2,2048,256,1]{2,1,0,3:T(8,128)(2,1)S(1)} %bitcast.88, bf16[256,1,2,256]{3,0,2,1:T(8,128)(2,1)S(1)} %get-tuple-element.22, bf16[256,1,2,256]{3,0,2,1:T(8,128)(2,1)S(1)} %get-tuple-element.21), kind=kOutput, calls=%fused_computation.11 | convolution fusion | flops 1077673984 | bytes 8912896 | tf_op jit(solution)/shard_map/qrk,cpqk->cpr/dot_general | solution.py:74
  25.9 18.0 %reshape.354 = f32[16,16,2,32,2,32]{5,4,3,1,0,2:T(2,128)} reshape(f32[256,2,2048]{2,0,1:T(8,128)} %get-tuple-element.50) | data formatting | bytes 8388608 | tf_op jit(solution)/shard_map/reshape | solution.py:80
  43.9 13.9 %fusion.49 = (f32[16,16,1,32,2,32]{5,4,3,1,0,2:T(2,128)}, f32[16,16,1,32,2,32]{5,4,3,1,0,2:T(2,128)}) fusion(f32[16,16,2,32,2,32]{5,4,3,1,0,2:T(2,128)} %reshape.354), kind=kLoop, calls=%fused_computation.106 | loop fusion | bytes 8388608 | tf_op jit(solution)/shard_map/slice | solution.py:95
  58.0 8.1 %multiply_subtract_fusion = (f32[16,16,32,2,32]{4,2,1,0,3:T(8,128)S(1)}, f32[16,16,32,2,32]{4,2,1,0,3:T(8,128)S(1)}) fusion(f32[16,16,1,32,2,32]{5,4,3,1,0,2:T(2,128)} %get-tuple-element.13, f32[16,16,1,32,2,32]{5,4,3,1,0,2:T(2,128)} %get-tuple-element.12, f32[16,32,2]{1,0,2:T(8,128)S(1)} %copy.66, f32[16,32,2]{1,0,2:T(8,128)S(1)} %copy.63), kind=kLoop, calls=%fused_computation.6 | loop fusion | flops 3145728 | bytes 8396800 | tf_op jit(solution)/shard_map/sub | solution.py:95
  66.1 3.7 %multiply_reduce_fusion = (f32[16]{0:T(128)S(1)}, bf16[1,16,16,32,32]{4,3,2,1,0:T(8,128)(2,1)S(1)}, bf16[1,16,16,32,32]{4,3,2,1,0:T(8,128)(2,1)S(1)}) fusion(f32[16,16,32,2,32]{4,2,1,0,3:T(8,128)S(1)} %get-tuple-element.11, f32[16,16,32,2,32]{4,2,1,0,3:T(8,128)S(1)} %get-tuple-element.10), kind=kLoop, calls=%fused_computation.10 | loop fusion | flops 2359280 | bytes 5242944 | tf_op jit(solution)/shard_map/reduce_sum | solution.py:102
  70.7 3.9 %copy.67 = bf16[16,2,32,16,32]{4,3,2,1,0:T(8,128)(2,1)} copy(bf16[16,2,32,16,32]{4,2,3,0,1:T(8,128)(2,1)S(1)} %maximum_bitcast_fusion) | data formatting | bytes 2097152 | tf_op jit(solution)/shard_map/transpose | solution.py:105
  74.6 6.8 %reshape.355 = bf16[16,2,32,512]{3,2,1,0:T(8,128)(2,1)} reshape(bf16[16,2,32,16,32]{4,3,2,1,0:T(8,128)(2,1)} %copy.67) | data formatting | bytes 2097152 | tf_op jit(solution)/shard_map/reshape | solution.py:105
  81.4 7.4 %all-to-all-start = ((bf16[16,2,32,512]{3,2,1,0:T(8,128)(2,1)}), bf16[16,2,32,512]{3,2,1,0:T(8,128)(2,1)S(1)}, u32[]{:S(2)}, u32[]{:S(2)}) async-start(bf16[16,2,32,512]{3,2,1,0:T(8,128)(2,1)} %reshape.355), calls=%async_computation | async-start | bytes 2097152 | tf_op jit(solution)/shard_map/all_to_all | solution.py:108
  89.8 5.5 %subtract_convert_fusion = (bf16[64,64,512]{2,1,0:T(8,128)(2,1)}, bf16[64,64,512]{2,1,0:T(8,128)(2,1)}) fusion(f32[64,512]{1,0:T(8,128)S(1)} %get-tuple-element.9, f32[64,512]{1,0:T(8,128)S(1)} %get-tuple-element.8, f32[64,512]{1,0:T(8,128)S(1)} %get-tuple-element.7, f32[64,512]{1,0:T(8,128)S(1)} %get-tuple-element.6), kind=kLoop, calls=%fused_computation.7 | loop fusion | flops 16777216 | bytes 8912896 | tf_op jit(solution)/shard_map/convert_element_type | solution.py:43
  95.3 6.4 %copy.68 = bf16[4096,512]{0,1:T(8,128)(2,1)} copy(bf16[4096,512]{1,0:T(8,128)(2,1)} %bitcast.85) | data formatting | bytes 8388608 | tf_op jit(solution)/shard_map/convert_element_type | solution.py:44
  101.8 6.4 %copy.60 = bf16[4096,512]{0,1:T(8,128)(2,1)} copy(bf16[4096,512]{1,0:T(8,128)(2,1)} %bitcast.83) | data formatting | bytes 8388608 | tf_op jit(solution)/shard_map/convert_element_type | solution.py:43
  108.2 8.4 %reduce_sum.62 = f32[16,16,32,2,32]{4,3,2,1,0:T(2,128)} reshape(f32[256,2048]{1,0:T(8,128)S(1)} %get-tuple-element.49) | data formatting | bytes 4194304 | tf_op jit(solution)/shard_map/reduce_sum | solution.py:82
  116.6 13.0 %reduce_sum.63 = f32[16,16,32,2]{3,2,1,0:T(8,128)} reduce(f32[16,16,32,2,32]{4,3,2,1,0:T(2,128)} %reduce_sum.62, f32[]{:T(128)} %constant.21.clone.1), dimensions={4}, to_apply=%region_4.5 | reduce | flops 507904 | bytes 2162692 | tf_op jit(solution)/shard_map/reduce_sum | solution.py:82
  129.6 3.5 %copy.71 = f32[16,16,32,2]{2,1,3,0:T(8,128)S(1)} copy(f32[16,16,32,2]{3,2,1,0:T(8,128)} %reduce_sum.63) | data formatting | bytes 131072 | tf_op jit(solution)/shard_map/reduce_sum | solution.py:82
  135.4 8.4 %fusion.10 = f32[4096,512]{0,1:T(8,128)} fusion(bf16[4096,512]{1,0:T(8,128)(2,1)} %bitcast.86, bf16[512,512]{1,0:T(8,128)(2,1)S(1)} %bitcast_negate_fusion, bf16[512,512]{1,0:T(8,128)(2,1)S(1)} %bitcast.93, bf16[512,512]{1,0:T(8,128)(2,1)S(1)} %bitcast.91), kind=kOutput, calls=%fused_computation.29 | convolution fusion | flops 2689597440 | bytes 14155776 | tf_op jit(solution)/shard_map/dot_general | solution.py:122
  143.9 7.9 %fusion.52 = f32[4096,512]{0,1:T(8,128)} fusion(bf16[4096,512]{1,0:T(8,128)(2,1)} %bitcast.84, bf16[512,512]{1,0:T(8,128)(2,1)S(1)} %fusion.4), kind=kOutput, calls=%fused_computation.109 | convolution fusion | flops 2147483648 | bytes 13107200 | tf_op jit(solution)/shard_map/dot_general | solution.py:122
  151.8 10.1 %add_reduce_fusion = f32[4096]{0:T(1024)S(1)} fusion(bf16[4096,512]{0,1:T(8,128)(2,1)} %copy.68, f32[4096,512]{0,1:T(8,128)} %fusion.52, f32[4096,512]{0,1:T(8,128)} %fusion.10, bf16[4096,512]{0,1:T(8,128)(2,1)} %copy.60, bf16[4096,512]{1,0:T(8,128)(2,1)S(1)} %bitcast.87, bf16[512,512]{1,0:T(8,128)(2,1)S(1)} %fusion.4), kind=kOutput, calls=%fused_computation.3 | convolution fusion | flops 2162159616 | bytes 29900800 | tf_op jit(solution)/shard_map/dot_general | solution.py:125
  162.5 12.4 %all_to_all.17 = f32[16,1,336]{2,1,0:T(1,128)S(1)} all-to-all(f32[16,1,336]{2,1,0:T(1,128)S(1)} %copy.73), channel_id=1, replica_groups=mesh['grp'=2,'chan'=16] {'chan'}, dimensions={0} | all-to-all | bytes 43008 | tf_op jit(solution)/shard_map/all_to_all | solution.py:139
  (46 shorter events, 8.3 us)
Async XLA Ops:
  43.9 14.0 %copy-start.2 = (f32[16,64]{0,1:T(8,128)S(1)}, f32[16,64]{0,1:T(8,128)}, u32[]{:S(2)}) copy-start(f32[16,64]{0,1:T(8,128)} %fusion.29) | copy-start | bytes 12292
  43.9 14.0 %copy-start.1 = (f32[16,64]{0,1:T(8,128)S(1)}, f32[16,64]{0,1:T(8,128)}, u32[]{:S(2)}) copy-start(f32[16,64]{0,1:T(8,128)} %fusion.28) | copy-start | bytes 12292
  74.6 14.2 %copy-start.3 = (f32[2,512]{1,0:T(2,128)S(1)}, f32[2,512]{1,0:T(2,128)}, u32[]{:S(2)}) copy-start(f32[2,512]{1,0:T(2,128)} %param.10) | copy-start | bytes 12292
  81.4 53.1 %all-to-all-start = ((bf16[16,2,32,512]{3,2,1,0:T(8,128)(2,1)}), bf16[16,2,32,512]{3,2,1,0:T(8,128)(2,1)S(1)}, u32[]{:S(2)}, u32[]{:S(2)}) async-start(bf16[16,2,32,512]{3,2,1,0:T(8,128)(2,1)} %reshape.355), calls=%async_computation | async-start | bytes 2097152 | tf_op jit(solution)/shard_map/all_to_all | solution.py:108
  129.5 4.3 %copy-start.4 = (s32[16]{0:T(128)S(1)}, s32[16]{0:T(128)}, u32[]{:S(2)}) copy-start(s32[16]{0:T(128)} %param.14) | copy-start | bytes 196
  129.6 4.6 %copy-start.5 = (s32[16]{0:T(128)S(1)}, s32[16]{0:T(128)}, u32[]{:S(2)}) copy-start(s32[16]{0:T(128)} %param.15) | copy-start | bytes 196
  143.9 7.9 %copy-start = (bf16[64,64,512]{2,1,0:T(8,128)(2,1)S(1)}, bf16[64,64,512]{2,1,0:T(8,128)(2,1)}, u32[]{:S(2)}) copy-start(bf16[64,64,512]{2,1,0:T(8,128)(2,1)} %get-tuple-element.20) | copy-start | bytes 12582916

commit v2 on v1

v2 whole, which is shorter than its diff:
```python
import math

import jax
import jax.numpy as jnp
from jax import lax
from jax.experimental import pallas as pl
from jax.experimental.pallas import tpu as pltpu
from jax.sharding import PartitionSpec as P

CH = 256
AVG = 16
GROUPS = 16
SPEC = 32
TAPS = 16
SIDE = 64
PIX = 4096
NCAL = 256

highest = lax.Precision.HIGHEST


def dft_table(length):
    indices = jnp.arange(length, dtype=jnp.int32)
    products = indices[:, None] * indices[None, :] % length
    angles = products.astype(jnp.float32) * jnp.float32(2.0 * math.pi / length)
    scaling = jnp.float32(1.0 / math.sqrt(length))
    cosine = jnp.cos(angles) * scaling
    sine_part = jnp.sin(angles) * scaling
    upper_half = jnp.stack([cosine, sine_part], axis=1)
    lower_half = jnp.stack([-sine_part, cosine], axis=1)
    return jnp.stack([upper_half, lower_half], axis=1).astype(jnp.bfloat16)


def polyphase(voltage, fir_taps):
    length = fir_taps.shape[1]
    window = voltage.reshape(voltage.shape[0], voltage.shape[1], -1, length)
    summed = jnp.zeros((voltage.shape[0], voltage.shape[1], SPEC, length), jnp.float32)
    for tap_index in range(TAPS):
        summed = summed + window[:, :, tap_index : tap_index + SPEC, :].astype(
            jnp.float32
        ) * fir_taps[tap_index].astype(jnp.float32)
    return summed.astype(jnp.bfloat16)


LANES = 128
STEP = 8
HALF = 16


def channelise_kernel(volt_ref, taps_ref, table_ref, gain_ref, out_ref, power_ref, cross_ref, filt, spec):
    length = taps_ref.shape[2]
    in_dev = volt_ref.shape[1]
    st_dev = in_dev // 2
    row_blocks = in_dev // HALF
    lane_blocks = length // LANES
    power_ref[...] = jnp.zeros_like(power_ref)
    cross_ref[...] = jnp.zeros_like(cross_ref)

    @pl.loop(0, SPEC // STEP)
    def _(block):
        first = block * STEP

        @pl.loop(0, 2 * row_blocks * lane_blocks)
        def _(turn):
            part = turn // (row_blocks * lane_blocks)
            row = pl.multiple_of(turn // lane_blocks % row_blocks * HALF, HALF)
            lane = pl.multiple_of(turn % lane_blocks * LANES, LANES)
            sums = [[None, None] for _ in range(STEP)]
            taps = [taps_ref[t, :, pl.ds(lane, LANES)] for t in range(TAPS)]
            for window in range(STEP + TAPS - 1):
                start = pl.multiple_of((first + window) * length + lane, LANES)
                both = volt_ref[part, pl.ds(row, HALF), pl.ds(start, LANES)].astype(jnp.float32)
                for half in range(2):
                    value = both[half * 8 : half * 8 + 8]
                    for s in range(max(0, window - TAPS + 1), min(STEP, window + 1)):
                        term = value * taps[window - s]
                        sums[s][half] = term if sums[s][half] is None else sums[s][half] + term
            column = pl.multiple_of(part * length + lane, LANES)
            for s in range(STEP):
                filt[s, pl.ds(row, HALF), pl.ds(column, LANES)] = jnp.concatenate(
                    sums[s], axis=0
                ).astype(jnp.bfloat16)

        rows = filt[...].reshape(STEP * in_dev, 2 * length)
        for column in range(2 * lane_blocks):
            product = jnp.dot(
                rows,
                table_ref[:, column * LANES : (column + 1) * LANES],
                preferred_element_type=jnp.float32,
            )
            spec[column] = product.astype(jnp.bfloat16).astype(jnp.float32)

        chunk = lax.broadcasted_iota(jnp.int32, (HALF, LANES), 1) // AVG
        for j in range(lane_blocks):
            lanes = slice(j * LANES, (j + 1) * LANES)
            for h in range(st_dev // HALF):
                st_rows = slice(h * HALF, (h + 1) * HALF)
                gre0, gim0, gre1, gim1 = (gain_ref[n, st_rows, lanes] for n in range(4))
                reals, imags = [], []
                power0 = power_ref[0, st_rows, lanes]
                power1 = power_ref[1, st_rows, lanes]
                cross = cross_ref[st_rows, lanes]
                for s in range(STEP):
                    base = s * in_dev + h * 2 * HALF
                    re0 = spec[j, pl.ds(base, HALF, stride=2), :]
                    re1 = spec[j, pl.ds(base + 1, HALF, stride=2), :]
                    im0 = spec[lane_blocks + j, pl.ds(base, HALF, stride=2), :]
                    im1 = spec[lane_blocks + j, pl.ds(base + 1, HALF, stride=2), :]
                    power0 = power0 + (re0 * re0 + im0 * im0)
                    power1 = power1 + (re1 * re1 + im1 * im1)
                    cre0 = re0 * gre0 - im0 * gim0
                    cim0 = re0 * gim0 + im0 * gre0
                    cre1 = re1 * gre1 - im1 * gim1
                    cim1 = re1 * gim1 + im1 * gre1
                    cross = cross + (cre0 * cre1 + cim0 * cim1)
                    reals.append(cre0 + cre1)
                    imags.append(cim0 + cim1)
                power_ref[0, st_rows, lanes] = power0
                power_ref[1, st_rows, lanes] = power1
                cross_ref[st_rows, lanes] = cross
                for q, planes in enumerate((reals, imags)):
                    bit = 1
                    while bit < STEP:
                        keep = (chunk // bit) % 2 == 0
                        for s in range(STEP):
                            if s & bit:
                                continue
                            low, high = planes[s], planes[s + bit]
                            shift = bit * AVG
                            planes[s] = jnp.where(keep, low, pltpu.roll(high, shift, 1))
                            planes[s + bit] = jnp.where(keep, pltpu.roll(low, LANES - shift, 1), high)
                        bit *= 2
                    where = pl.ds(pl.multiple_of(block * LANES, LANES), LANES)
                    for d in range(STEP):
                        out_ref[j * STEP + d, q, st_rows, where] = planes[d].astype(jnp.bfloat16)


def image_kernel(data_ref, steer_ref, out_ref, even_ref, odd_ref, along, turned):
    stations, depth = data_ref.shape[1], data_ref.shape[2]
    along[:, :depth] = data_ref[0]
    along[:, depth:] = data_ref[1]
    turned[:, :depth] = data_ref[1]
    turned[:, depth:] = -data_ref[0]
    contract = (((1,), (1,)), ((), ()))
    tall = 256

    @pl.loop(0, stations // tall)
    def _(block):
        rows = pl.ds(pl.multiple_of(block * tall, tall), tall)
        even = lax.dot_general(along[rows, :], along[...], contract, preferred_element_type=jnp.float32)
        odd = lax.dot_general(turned[rows, :], along[...], contract, preferred_element_type=jnp.float32)
        row_ids = lax.broadcasted_iota(jnp.int32, (tall, stations), 0) + block * tall
        same = row_ids == lax.broadcasted_iota(jnp.int32, (tall, stations), 1)
        even_ref[rows, :] = jnp.where(same, 0.0, even).astype(jnp.bfloat16)
        odd_ref[rows, :] = jnp.where(same, 0.0, -2.0 * odd).astype(jnp.bfloat16)

    tile = out_ref.shape[1]
    lines = tile // SIDE

    @pl.loop(0, out_ref.shape[0])
    def _(block):
        cosines, sines = [], []
        for line in range(lines):
            u = block * lines + line
            east_cos = steer_ref[0, pl.ds(u, 1), :]
            east_sin = steer_ref[1, pl.ds(u, 1), :]
            cosines.append(east_cos * steer_ref[2] - east_sin * steer_ref[3])
            sines.append(east_sin * steer_ref[2] + east_cos * steer_ref[3])
        cosine = jnp.concatenate(cosines, axis=0)
        sine = jnp.concatenate(sines, axis=0)
        cos16, sin16 = cosine.astype(jnp.bfloat16), sine.astype(jnp.bfloat16)
        first = jnp.dot(cos16, even_ref[...], preferred_element_type=jnp.float32)
        first = first + jnp.dot(sin16, odd_ref[...], preferred_element_type=jnp.float32)
        second = jnp.dot(sin16, even_ref[...], preferred_element_type=jnp.float32)
        terms = cosine * first + sine * second
        folded = terms[:, :LANES]
        for j in range(1, stations // LANES):
            folded = folded + terms[:, j * LANES : (j + 1) * LANES]
        out_ref[pl.ds(block, 1), :] = jnp.sum(folded.T, axis=0, keepdims=True)


def beam_images(joined, positions):
    steps = (jnp.arange(SIDE, dtype=jnp.float32) - SIDE // 2) / jnp.float32(SIDE)
    phases = jnp.float32(2.0 * math.pi) * (positions[:, None, :] * steps[None, :, None])
    steer = jnp.stack([jnp.cos(phases), jnp.sin(phases)], axis=1).reshape(
        4, SIDE, positions.shape[1]
    )
    stations, depth = joined.shape[1], joined.shape[2]
    vmem = pl.BlockSpec(memory_space=pltpu.VMEM)
    return pl.pallas_call(
        image_kernel,
        out_shape=jax.ShapeDtypeStruct((PIX // 256, 256), jnp.float32),
        in_specs=[vmem, vmem],
        out_specs=vmem,
        scratch_shapes=[
            pltpu.VMEM((stations, stations), jnp.bfloat16),
            pltpu.VMEM((stations, stations), jnp.bfloat16),
            pltpu.VMEM((stations, 2 * depth), jnp.bfloat16),
            pltpu.VMEM((stations, 2 * depth), jnp.bfloat16),
        ],
        compiler_params=pltpu.CompilerParams(vmem_limit_bytes=32 * 1024 * 1024),
        name="beam_images",
    )(joined, steer)


def channelise(voltages, fir_taps, gain_re, gain_im):
    in_dev = voltages.shape[1]
    st_dev = in_dev // 2
    table = jnp.transpose(dft_table(CH), (2, 3, 1, 0)).reshape(2 * CH, 2 * CH)
    taps = jnp.broadcast_to(fir_taps.astype(jnp.float32)[:, None], (TAPS, 8, CH))
    both = jnp.stack([gain_re, gain_im]).reshape(2, GROUPS, st_dev, 2)
    gains = jnp.repeat(jnp.transpose(both, (3, 0, 2, 1)).reshape(4, st_dev, GROUPS), AVG, axis=2)
    vmem = pl.BlockSpec(memory_space=pltpu.VMEM)
    return pl.pallas_call(
        channelise_kernel,
        out_shape=[
            jax.ShapeDtypeStruct((GROUPS, 2, st_dev, AVG * SPEC), jnp.bfloat16),
            jax.ShapeDtypeStruct((2, st_dev, CH), jnp.float32),
            jax.ShapeDtypeStruct((st_dev, CH), jnp.float32),
        ],
        in_specs=[vmem] * 4,
        out_specs=[vmem] * 3,
        scratch_shapes=[
            pltpu.VMEM((STEP, in_dev, 2 * CH), jnp.bfloat16),
            pltpu.VMEM((2 * CH // LANES, STEP * in_dev, LANES), jnp.float32),
        ],
        compiler_params=pltpu.CompilerParams(vmem_limit_bytes=32 * 1024 * 1024),
        name="channelise",
    )(voltages, taps, table, gains)


def channelise_small(voltages, fir_taps, gain_re, gain_im, chan_dev):
    in_dev = voltages.shape[1]
    st_dev = in_dev // 2
    spectra = jnp.einsum(
        "qrk,cpqk->cpr",
        polyphase(voltages, fir_taps).reshape(2, in_dev * SPEC, CH),
        dft_table(CH),
        preferred_element_type=jnp.float32,
    ).astype(jnp.bfloat16)
    values = spectra.astype(jnp.float32).reshape(GROUPS, AVG, 2, st_dev, 2, SPEC)
    powers = jnp.sum(values * values, axis=(2, 5)).reshape(CH, st_dev, 2)
    gre = gain_re.reshape(GROUPS, 1, st_dev, 2, 1)
    gim = gain_im.reshape(GROUPS, 1, st_dev, 2, 1)
    cal_re = values[:, :, 0] * gre - values[:, :, 1] * gim
    cal_im = values[:, :, 0] * gim + values[:, :, 1] * gre
    sums = jnp.stack(
        [cal_re[:, :, :, 0] + cal_re[:, :, :, 1], cal_im[:, :, :, 0] + cal_im[:, :, :, 1]]
    ).astype(jnp.bfloat16)
    crossed = cal_re[:, :, :, 0] * cal_re[:, :, :, 1] + cal_im[:, :, :, 0] * cal_im[:, :, :, 1]
    cross = jnp.sum(crossed, axis=3).reshape(CH, st_dev).T
    sums = jnp.transpose(
        sums.reshape(2, CH // chan_dev, chan_dev, st_dev, SPEC), (1, 0, 3, 2, 4)
    ).reshape(CH // chan_dev, 2, st_dev, chan_dev * SPEC)
    return sums, jnp.transpose(powers, (2, 1, 0)), cross


def local(voltages, fir_taps, positions, cal_amp, cal_phase, cal_index, owner_counts, tile_owner):
    devices = lax.axis_size("chan")
    myself = lax.axis_index("chan")
    in_dev = voltages.shape[1]
    st_dev = in_dev // 2
    stations = st_dev * devices
    chan_dev = CH // devices
    per_group = AVG // chan_dev

    my_index = lax.dynamic_slice_in_dim(cal_index, myself * in_dev, in_dev, 0)
    selection = (my_index[:, None] == jnp.arange(NCAL, dtype=jnp.int32)[None, :]).astype(jnp.float32)
    gain_re = jnp.dot(selection, cal_amp * jnp.cos(cal_phase), precision=highest).T
    gain_im = jnp.dot(selection, cal_amp * jnp.sin(cal_phase), precision=highest).T

    if chan_dev == AVG and st_dev % HALF == 0:
        outgoing, powers, crosses = channelise(voltages, fir_taps, gain_re, gain_im)
    else:
        outgoing, powers, crosses = channelise_small(voltages, fir_taps, gain_re, gain_im, chan_dev)
    incoming = lax.all_to_all(outgoing, "chan", split_axis=0, concat_axis=0, tiled=True)


    power_rows = jnp.transpose(powers, (2, 1, 0)).reshape(CH, in_dev) / jnp.float32(SPEC)
    offsets = jnp.cumsum(owner_counts) - owner_counts
    chan_ids = jnp.arange(CH, dtype=jnp.int32)
    member = (
        (chan_ids[None, :] >= offsets[:, None])
        & (chan_ids[None, :] < (offsets + owner_counts)[:, None])
    ).astype(jnp.float32)
    divisor = jnp.maximum(owner_counts, 1).astype(jnp.float32)
    sub_rows = jnp.dot(member, power_rows, precision=highest) / divisor[:, None]

    cross_power = 2.0 * jnp.sum(crosses.reshape(st_dev, GROUPS, AVG), axis=(0, 2))
    joined = jnp.transpose(incoming, (1, 0, 2, 3)).reshape(2, stations, chan_dev * SPEC)
    image = beam_images(joined, positions)

    tile_pix = PIX // devices
    device_ids = jnp.arange(devices, dtype=jnp.int32)
    tile_of = jnp.sum(
        jnp.where(tile_owner[None, :] == device_ids[:, None], device_ids[None, :], 0), axis=1
    )
    tiles = image.reshape(devices, tile_pix)[tile_of]
    last = jnp.concatenate(
        [tiles, sub_rows, jnp.broadcast_to(cross_power[None], (devices, GROUPS))], axis=1
    )
    arrived = lax.all_to_all(last, "chan", split_axis=0, concat_axis=0, tiled=True)
    scale = jnp.float32(1.0 / (SPEC * AVG) * math.sqrt(SPEC * AVG) / (2 * stations))
    pieces = jnp.sum(arrived[:, :tile_pix].reshape(GROUPS, per_group, tile_pix), axis=1)
    constant = jnp.sum(arrived[:, tile_pix + in_dev :], axis=0)
    result = scale * (pieces + constant[:, None])
    autos = arrived[:, tile_pix : tile_pix + in_dev].reshape(1, devices * in_dev)
    return (result[None], autos)


def solution(mesh):
    in_specs = (
        P(None, ("grp", "chan"), None),
        P(),
        P(),
        P("grp", None),
        P("grp", None),
        P(),
        P("grp"),
        P("grp"),
    )
    out_specs = (P(("grp", "chan"), None, None), P(("grp", "chan"), None))
    return jax.shard_map(local, mesh=mesh, in_specs=in_specs, out_specs=out_specs, check_vma=False)
```

time: 177 us -> 84 us (0.47)
  local copies, waits for them, and re-layouts: 75 us -> 8.72 us
  other arithmetic: 46.9 us -> 6.84 us
  matrix products: 33.9 us -> 2.25 us
  Pallas kernels: 0 us -> 23.4 us
  waiting for transfers between devices: 0.02 us -> 20.9 us
    dot_general x5 -> x0, matrix products: 30.6 us -> none  [the longest x1 10.1 us: local(): second = jnp.dot(sine, even, preferred_element_type=jnp.float32)]
    reshape x4 -> x1, local copies, waits for them, and re-layouts: 29.2 us -> 1.21 us  [channelise(): jnp.repeat(jnp.transpose(both, (3, 0, 2, 1)).reshape(4, st_dev, GROUPS),...]
    pallas_call x0 -> x2, Pallas kernels: none -> 23.4 us  [the longest x1 12.3 us: beam_images(): pl.pallas_call(image_kernel, out_shape=jax.ShapeDtypeStruct((PIX // 256,...]
    all_to_all x1, waiting for transfers between devices: 0.02 us -> 20.9 us  [local(): lax.all_to_all(outgoing, 'chan', split_axis=0, concat_axis=0, tiled=True)]
    convert_element_type x3 -> x0, other arithmetic: 16.9 us -> none  [the longest x1 9.7 us: polyphase(): return summed.astype(jnp.bfloat16)]
    reduce_sum x2, other arithmetic: 16.7 us -> 0.14 us  [local(): jnp.sum(crosses.reshape(st_dev, GROUPS, AVG), axis=(0, 2))]
    slice x3 -> x0, local copies, waits for them, and re-layouts: 14.1 us -> none  [the longest x1 13.9 us: local(): cal_re = values[:, :, 0] * gre - values[:, :, 1] * gim]
    convert_element_type x2 -> x0, local copies, waits for them, and re-layouts: 12.8 us -> none  [the longest x1 6.43 us: steering_tables(): sine.reshape(PIX, stations).astype(jnp.bfloat16)]
  transfers between devices with their start and end apart: 1 -> 1, of which waited for: 0 -> 1; matrix products, arithmetic and copies ran while one was open for 26% -> 2% of each run, Pallas kernels for 0% -> 0%
where the time goes in v2:
time: 84 us; the launch traced here: 83.5 us
  Pallas kernels  23.4 us (28%)
  waiting for transfers between devices  20.9 us (25%)
  blocking collectives  13.2 us (16%)
  local copies, waits for them, and re-layouts  8.72 us (10%)
  starting transfers between devices  7.39 us (9%)
  other arithmetic  6.84 us (8%)
  matrix products  2.25 us (3%)
  between operations  0.87 us (1%)
    all_to_all x1, waiting for transfers between devices, local(): lax.all_to_all(outgoing, 'chan', split_axis=0, concat_axis=0, tiled=True)  20.9 us
    all_to_all x1, blocking collectives, local(): lax.all_to_all(last, 'chan', split_axis=0, concat_axis=0, tiled=True)  13.2 us
    pallas_call x1, Pallas kernels, beam_images(): pl.pallas_call(image_kernel, out_shape=jax.ShapeDtypeStruct((PIX // 256,...  12.3 us
    pallas_call x1, Pallas kernels, channelise(): pl.pallas_call(channelise_kernel, out_shape=[jax.ShapeDtypeStruct((GROUPS...  11.1 us
    all_to_all x1, starting transfers between devices, local(): lax.all_to_all(outgoing, 'chan', split_axis=0, concat_axis=0, tiled=True)  7.39 us
    another operation x4, other arithmetic  2.91 us
    unnamed x14, local copies, waits for them, and re-layouts  2.14 us
    transpose x1, local copies, waits for them, and re-layouts, channelise(): table = jnp.transpose(dft_table(CH), (2, 3, 1, 0)).reshape(2 * CH, 2 * CH)  2.01 us
  transfers between devices with their start and end apart: 1, of which 1 were waited for; matrix products, arithmetic and copies ran while one was open for 2% of the time, Pallas kernels for 0%

profile of v2, /device:TPU:0, one launch (start us, length us, event | category | flops | bytes accessed | tf_op | source)
XLA Modules:
  0.0 83.5 jit_solution(6214652272696599166)
XLA Ops:
  0.6 0.8 dynamic_slice.3
  1.4 1.1 %fusion.10 = f32[16,64]{0,1:T(8,128)S(1)} fusion(s32[64]{0:T(128)S(1)} %dynamic_slice.3, f32[256,16]{0,1:T(8,128)} %param.11, f32[256,16]{0,1:T(8,128)} %param.12), kind=kOutput, calls=%fused_computation.26 | convolution fusion | flops 3166208 | bytes 37120 | tf_op jit(solution)/shard_map/dot_general | solution.py:269
  2.5 1.0 %fusion.9 = f32[16,64]{0,1:T(8,128)S(1)} fusion(s32[64]{0:T(128)S(1)} %dynamic_slice.3, f32[256,16]{0,1:T(8,128)} %param.11, f32[256,16]{0,1:T(8,128)} %param.12), kind=kOutput, calls=%fused_computation.25 | convolution fusion | flops 3166208 | bytes 37120 | tf_op jit(solution)/shard_map/dot_general | solution.py:270
  3.5 1.1 %negate_convert_fusion = (bf16[256,1,256]{2,0,1:T(8,128)(2,1)S(1)}, bf16[256,1,256]{2,0,1:T(8,128)(2,1)S(1)}) fusion(), kind=kLoop, calls=%fused_computation.15 | loop fusion | flops 1245184 | bytes 262144 | tf_op jit(solution)/shard_map/convert.3
  4.6 1.6 %fusion.8 = bf16[256,1,256]{2,0,1:T(8,128)(2,1)} fusion(), kind=kLoop, calls=%fused_computation.21 | loop fusion | flops 1048576 | bytes 131072 | tf_op jit(solution)/shard_map/convert.7
  6.4 0.8 broadcast_in_dim.15
  7.2 1.2 %copy.34.gain_ref = f32[4,32,256]{2,1,0:T(8,128)S(1)} copy(f32[4,32,256]{1,2,0:T(8,128)} %bitcast.39) | data formatting | bytes 262144 | tf_op jit(solution)/shard_map/reshape | solution.py:212
  8.4 1.0 %maximum_bitcast_fusion.1 = (bf16[256,1,2,256]{3,0,2,1:T(8,128)(2,1)S(1)}, bf16[256,1,2,256]{3,0,2,1:T(8,128)(2,1)S(1)}) fusion(bf16[256,1,256]{2,0,1:T(8,128)(2,1)} %fusion.8, bf16[256,1,256]{2,0,1:T(8,128)(2,1)S(1)} %get-tuple-element.15, bf16[256,1,256]{2,0,1:T(8,128)(2,1)S(1)} %get-tuple-element.14), kind=kLoop, calls=%fused_computation.10 | loop fusion | flops 262144 | bytes 917504 | tf_op jit(solution)/shard_map/stack | solution.py:31
  9.4 0.8 %maximum_bitcast_fusion = bf16[2,256,2,256]{1,3,0,2:T(8,128)(2,1)} fusion(bf16[256,1,2,256]{3,0,2,1:T(8,128)(2,1)S(1)} %get-tuple-element.9, bf16[256,1,2,256]{3,0,2,1:T(8,128)(2,1)S(1)} %get-tuple-element.8), kind=kLoop, calls=%fused_computation.2 | loop fusion | flops 262144 | bytes 1048576 | tf_op jit(solution)/shard_map/transpose | solution.py:209
  10.2 2.0 %copy.30 = bf16[2,256,2,256]{3,2,1,0:T(2,128)(2,1)} copy(bf16[2,256,2,256]{1,3,0,2:T(8,128)(2,1)} %maximum_bitcast_fusion) | data formatting | bytes 1048576 | tf_op jit(solution)/shard_map/transpose | solution.py:209
  12.2 1.1 %copy.42 = bf16[64,8,2,256]{3,1,2,0:T(8,128)(2,1)S(1)} copy(bf16[64,8,2,256]{3,2,1,0:T(2,128)(2,1)} %bitcast.40) | data formatting | bytes 1048576
  13.4 11.1 %channelise.1 = (bf16[16,2,32,512]{3,2,1,0:T(8,128)(2,1)S(1)}, f32[2,32,256]{2,1,0:T(8,128)S(1)}, f32[32,256]{1,0:T(8,128)S(1)}) custom-call(bf16[2,64,12032]{2,1,0:T(8,128)(2,1)S(1)} %copy-done, f32[16,8,256]{2,1,0:T(8,128)S(1)} %broadcast_in_dim.14.taps_ref, bf16[512,512]{1,0:T(8,128)(2,1)S(1)} %bitcast.37, f32[4,32,256]{2,1,0:T(8,128)S(1)} %copy.34.gain_ref), custom_call_target="tpu_custom_call" | custom-call | tf_op jit(solution)/shard_map/channelise/pallas_call | solution.py:214
  24.5 1.0 %copy-done.1 = bf16[16,2,32,512]{3,2,1,0:T(8,128)(2,1)} copy-done((bf16[16,2,32,512]{3,2,1,0:T(8,128)(2,1)}, bf16[16,2,32,512]{3,2,1,0:T(8,128)(2,1)S(1)}, u32[]{:S(2)}) %copy-start.1) | copy-done | bytes 1048600
  25.5 7.4 %all-to-all-start = ((bf16[16,2,32,512]{3,2,1,0:T(8,128)(2,1)}), bf16[16,2,32,512]{3,2,1,0:T(8,128)(2,1)S(1)}, u32[]{:S(2)}, u32[]{:S(2)}) async-start(bf16[16,2,32,512]{3,2,1,0:T(8,128)(2,1)} %copy-done.1), calls=%async_computation | async-start | bytes 2097152 | tf_op jit(solution)/shard_map/all_to_all | solution.py:276
  33.2 0.1 reduce.2
  33.4 0.1 reduce_sum.44
  33.8 1.0 %fusion.4 = (f32[2,1,64,512]{3,2,1,0:T(8,128)S(1)}, f32[2,1,64,512]{3,2,1,0:T(8,128)S(1)}) fusion(f32[64]{0:T(128)S(1)} %add_multiply_fusion, f32[2,512]{1,0:T(2,128)S(1)} %copy-done.3), kind=kLoop, calls=%fused_computation.14 | loop fusion | flops 131072 | bytes 528640 | tf_op jit(solution)/shard_map/cos | solution.py:185
  34.8 0.2 convolution_divide_fusion
  35.0 20.9 %all-to-all-done = bf16[16,2,32,512]{3,2,1,0:T(8,128)(2,1)S(1)} async-done(((bf16[16,2,32,512]{3,2,1,0:T(8,128)(2,1)}), bf16[16,2,32,512]{3,2,1,0:T(8,128)(2,1)S(1)}, u32[]{:S(2)}, u32[]{:S(2)}) %all-to-all-start) | async-done | bytes 1048608 | tf_op jit(solution)/shard_map/all_to_all | solution.py:276
  55.9 12.3 %beam_images.1 = f32[16,256]{1,0:T(8,128)S(1)} custom-call(bf16[2,512,512]{2,1,0:T(8,128)(2,1)S(1)} %bitcast.35, f32[4,64,512]{2,1,0:T(8,128)S(1)} %bitcast.36), custom_call_target="tpu_custom_call" | custom-call | tf_op jit(solution)/shard_map/beam_images/pallas_call | solution.py:190
  68.2 0.6 gather_fusion
  68.8 13.2 %all_to_all.17 = f32[16,1,336]{2,1,0:T(1,128)S(1)} all-to-all(f32[16,1,336]{2,1,0:T(1,128)S(1)} %copy.38), channel_id=1, replica_groups=mesh['grp'=2,'chan'=16] {'chan'}, dimensions={0} | all-to-all | bytes 43008 | tf_op jit(solution)/shard_map/all_to_all | solution.py:302
  82.2 0.7 fusion.14
  82.8 0.7 reshape.195
  (35 shorter events, 0.9 us)
Async XLA Ops:
  0.6 12.7 %copy-start.2 = (bf16[16,256]{1,0:T(8,128)(2,1)S(1)}, bf16[16,256]{1,0:T(8,128)(2,1)}, u32[]{:S(2)}) copy-start(bf16[16,256]{1,0:T(8,128)(2,1)} %param.9) | copy-start | bytes 24580
  1.4 12.0 %copy-start = (bf16[2,64,12032]{2,1,0:T(8,128)(2,1)S(1)}, bf16[2,64,12032]{2,1,0:T(8,128)(2,1)}, u32[]{:S(2)}) copy-start(bf16[2,64,12032]{2,1,0:T(8,128)(2,1)} %volt_ref.1) | copy-start | bytes 9240580
  13.4 19.6 %copy-start.4 = (s32[16]{0:T(128)S(1)}, s32[16]{0:T(128)}, u32[]{:S(2)}) copy-start(s32[16]{0:T(128)} %param.14) | copy-start | bytes 196
  13.4 20.2 %copy-start.5 = (s32[16]{0:T(128)S(1)}, s32[16]{0:T(128)}, u32[]{:S(2)}) copy-start(s32[16]{0:T(128)} %param.15) | copy-start | bytes 196
  13.4 20.3 %copy-start.3 = (f32[2,512]{1,0:T(2,128)S(1)}, f32[2,512]{1,0:T(2,128)}, u32[]{:S(2)}) copy-start(f32[2,512]{1,0:T(2,128)} %param.10) | copy-start | bytes 12292
  24.5 1.0 %copy-start.1 = (bf16[16,2,32,512]{3,2,1,0:T(8,128)(2,1)}, bf16[16,2,32,512]{3,2,1,0:T(8,128)(2,1)S(1)}, u32[]{:S(2)}) copy-start(bf16[16,2,32,512]{3,2,1,0:T(8,128)(2,1)S(1)} %get-tuple-element.5) | copy-start | bytes 3145732
  25.5 30.3 %all-to-all-start = ((bf16[16,2,32,512]{3,2,1,0:T(8,128)(2,1)}), bf16[16,2,32,512]{3,2,1,0:T(8,128)(2,1)S(1)}, u32[]{:S(2)}, u32[]{:S(2)}) async-start(bf16[16,2,32,512]{3,2,1,0:T(8,128)(2,1)} %copy-done.1), calls=%async_computation | async-start | bytes 2097152 | tf_op jit(solution)/shard_map/all_to_all | solution.py:276

commit v3 on v2

--- a/solution.py
+++ b/solution.py
@@ -1,6 +1,7 @@
 import math
 
 import jax
+import numpy as np
 import jax.numpy as jnp
 from jax import lax
 from jax.experimental import pallas as pl
@@ -20,15 +21,13 @@
 
 
 def dft_table(length):
-    indices = jnp.arange(length, dtype=jnp.int32)
-    products = indices[:, None] * indices[None, :] % length
-    angles = products.astype(jnp.float32) * jnp.float32(2.0 * math.pi / length)
-    scaling = jnp.float32(1.0 / math.sqrt(length))
-    cosine = jnp.cos(angles) * scaling
-    sine_part = jnp.sin(angles) * scaling
-    upper_half = jnp.stack([cosine, sine_part], axis=1)
-    lower_half = jnp.stack([-sine_part, cosine], axis=1)
-    return jnp.stack([upper_half, lower_half], axis=1).astype(jnp.bfloat16)
+    indices = np.arange(length, dtype=np.int64)
+    angles = (indices[:, None] * indices[None, :] % length) * (2.0 * math.pi / length)
+    cosine = np.cos(angles) / math.sqrt(length)
+    sine_part = np.sin(angles) / math.sqrt(length)
+    upper_half = np.stack([cosine, sine_part], axis=1)
+    lower_half = np.stack([-sine_part, cosine], axis=1)
+    return np.stack([upper_half, lower_half], axis=1).astype(jnp.bfloat16)
 
 
 def polyphase(voltage, fir_taps):
@@ -47,14 +46,38 @@
 HALF = 16
 
 
-def channelise_kernel(volt_ref, taps_ref, table_ref, gain_ref, out_ref, power_ref, cross_ref, filt, spec):
-    length = taps_ref.shape[2]
+def channelise_kernel(
+    volt_ref, fir_ref, table_ref, index_ref, solution_ref, out_ref, power_ref, cross_ref,
+    filt, spec, taps_ref, gain_ref,
+):
+    length = fir_ref.shape[1]
     in_dev = volt_ref.shape[1]
     st_dev = in_dev // 2
     row_blocks = in_dev // HALF
     lane_blocks = length // LANES
     power_ref[...] = jnp.zeros_like(power_ref)
     cross_ref[...] = jnp.zeros_like(cross_ref)
+    fir = fir_ref[...].astype(jnp.float32)
+    for t in range(TAPS):
+        taps_ref[t] = jnp.broadcast_to(fir[t : t + 1], (8, length))
+    group_ids = lax.broadcasted_iota(jnp.int32, (GROUPS, length), 0)
+    spread = (
+        group_ids == lax.broadcasted_iota(jnp.int32, (GROUPS, length), 1) // AVG
+    ).astype(jnp.float32)
+    solution_ids = lax.broadcasted_iota(jnp.int32, (NCAL, st_dev), 0)
+    for pol in range(2):
+        chosen = (solution_ids == index_ref[pol : pol + 1, :]).astype(jnp.float32)
+        for q in range(2):
+            picked = lax.dot_general(
+                chosen,
+                solution_ref[q],
+                (((0,), (0,)), ((), ())),
+                precision=highest,
+                preferred_element_type=jnp.float32,
+            )
+            gain_ref[pol * 2 + q] = jnp.dot(
+                picked, spread, precision=highest, preferred_element_type=jnp.float32
+            )
 
     @pl.loop(0, SPEC // STEP)
     def _(block):
@@ -155,19 +178,11 @@
         odd_ref[rows, :] = jnp.where(same, 0.0, -2.0 * odd).astype(jnp.bfloat16)
 
     tile = out_ref.shape[1]
-    lines = tile // SIDE
-
-    @pl.loop(0, out_ref.shape[0])
+
+    @pl.loop(0, out_ref.shape[0], unroll=2)
     def _(block):
-        cosines, sines = [], []
-        for line in range(lines):
-            u = block * lines + line
-            east_cos = steer_ref[0, pl.ds(u, 1), :]
-            east_sin = steer_ref[1, pl.ds(u, 1), :]
-            cosines.append(east_cos * steer_ref[2] - east_sin * steer_ref[3])
-            sines.append(east_sin * steer_ref[2] + east_cos * steer_ref[3])
-        cosine = jnp.concatenate(cosines, axis=0)
-        sine = jnp.concatenate(sines, axis=0)
+        pixels = pl.ds(pl.multiple_of(block * tile, tile), tile)
+        cosine, sine = steer_ref[0, pixels, :], steer_ref[1, pixels, :]
         cos16, sin16 = cosine.astype(jnp.bfloat16), sine.astype(jnp.bfloat16)
         first = jnp.dot(cos16, even_ref[...], preferred_element_type=jnp.float32)
         first = first + jnp.dot(sin16, odd_ref[...], preferred_element_type=jnp.float32)
@@ -179,12 +194,36 @@
         out_ref[pl.ds(block, 1), :] = jnp.sum(folded.T, axis=0, keepdims=True)
 
 
-def beam_images(joined, positions):
+def steering_kernel(axis_ref, out_ref):
+    @pl.loop(0, SIDE)
+    def _(u):
+        east_cos = axis_ref[0, pl.ds(u, 1), :]
+        east_sin = axis_ref[1, pl.ds(u, 1), :]
+        pixels = pl.ds(pl.multiple_of(u * SIDE, SIDE), SIDE)
+        out_ref[0, pixels, :] = east_cos * axis_ref[2] - east_sin * axis_ref[3]
+        out_ref[1, pixels, :] = east_sin * axis_ref[2] + east_cos * axis_ref[3]
+
+
+def steering_tables(positions):
     steps = (jnp.arange(SIDE, dtype=jnp.float32) - SIDE // 2) / jnp.float32(SIDE)
     phases = jnp.float32(2.0 * math.pi) * (positions[:, None, :] * steps[None, :, None])
-    steer = jnp.stack([jnp.cos(phases), jnp.sin(phases)], axis=1).reshape(
-        4, SIDE, positions.shape[1]
-    )
+    stations = positions.shape[1]
+    axes = jnp.stack([jnp.cos(phases), jnp.sin(phases)], axis=1).reshape(4, SIDE, stations)
+    vmem = pl.BlockSpec(memory_space=pltpu.VMEM)
+    return pl.pallas_call(
+        steering_kernel,
+        out_shape=jax.ShapeDtypeStruct((2, PIX, stations), jnp.float32),
+        in_specs=[vmem],
+        out_specs=vmem,
+        cost_estimate=pl.CostEstimate(
+            flops=6 * PIX * stations, bytes_accessed=8 * PIX * stations, transcendentals=0
+        ),
+        compiler_params=pltpu.CompilerParams(vmem_limit_bytes=24 * 1024 * 1024),
+        name="steering",
+    )(axes)
+
+
+def beam_images(joined, steer):
     stations, depth = joined.shape[1], joined.shape[2]
     vmem = pl.BlockSpec(memory_space=pltpu.VMEM)
     return pl.pallas_call(
@@ -198,18 +237,15 @@
             pltpu.VMEM((stations, 2 * depth), jnp.bfloat16),
             pltpu.VMEM((stations, 2 * depth), jnp.bfloat16),
         ],
-        compiler_params=pltpu.CompilerParams(vmem_limit_bytes=32 * 1024 * 1024),
+        compiler_params=pltpu.CompilerParams(vmem_limit_bytes=36 * 1024 * 1024),
         name="beam_images",
     )(joined, steer)
 
 
-def channelise(voltages, fir_taps, gain_re, gain_im):
+def channelise(voltages, fir_taps, my_index, solutions):
     in_dev = voltages.shape[1]
     st_dev = in_dev // 2
-    table = jnp.transpose(dft_table(CH), (2, 3, 1, 0)).reshape(2 * CH, 2 * CH)
-    taps = jnp.broadcast_to(fir_taps.astype(jnp.float32)[:, None], (TAPS, 8, CH))
-    both = jnp.stack([gain_re, gain_im]).reshape(2, GROUPS, st_dev, 2)
-    gains = jnp.repeat(jnp.transpose(both, (3, 0, 2, 1)).reshape(4, st_dev, GROUPS), AVG, axis=2)
+    table = jnp.asarray(np.transpose(dft_table(CH), (2, 3, 1, 0)).reshape(2 * CH, 2 * CH))
     vmem = pl.BlockSpec(memory_space=pltpu.VMEM)
     return pl.pallas_call(
         channelise_kernel,
@@ -218,18 +254,20 @@
             jax.ShapeDtypeStruct((2, st_dev, CH), jnp.float32),
             jax.ShapeDtypeStruct((st_dev, CH), jnp.float32),
         ],
-        in_specs=[vmem] * 4,
+        in_specs=[vmem] * 5,
         out_specs=[vmem] * 3,
         scratch_shapes=[
             pltpu.VMEM((STEP, in_dev, 2 * CH), jnp.bfloat16),
             pltpu.VMEM((2 * CH // LANES, STEP * in_dev, LANES), jnp.float32),
+            pltpu.VMEM((TAPS, 8, CH), jnp.float32),
+            pltpu.VMEM((4, st_dev, CH), jnp.float32),
         ],
         compiler_params=pltpu.CompilerParams(vmem_limit_bytes=32 * 1024 * 1024),
         name="channelise",
-    )(voltages, taps, table, gains)
-
-
-def channelise_small(voltages, fir_taps, gain_re, gain_im, chan_dev):
+    )(voltages, fir_taps, table, my_index, solutions)
+
+
+def channelise_small(voltages, fir_taps, my_index, solutions, chan_dev):
     in_dev = voltages.shape[1]
     st_dev = in_dev // 2
     spectra = jnp.einsum(
@@ -240,8 +278,9 @@
     ).astype(jnp.bfloat16)
     values = spectra.astype(jnp.float32).reshape(GROUPS, AVG, 2, st_dev, 2, SPEC)
     powers = jnp.sum(values * values, axis=(2, 5)).reshape(CH, st_dev, 2)
-    gre = gain_re.reshape(GROUPS, 1, st_dev, 2, 1)
-    gim = gain_im.reshape(GROUPS, 1, st_dev, 2, 1)
+    selection = (my_index.T[..., None] == jnp.arange(NCAL, dtype=jnp.int32)).astype(jnp.float32)
+    gains = jnp.einsum("kpn,qng->qgkp", selection, solutions, precision=highest)
+    gre, gim = gains[:, :, None, :, :, None]
     cal_re = values[:, :, 0] * gre - values[:, :, 1] * gim
     cal_im = values[:, :, 0] * gim + values[:, :, 1] * gre
     sums = jnp.stack(
@@ -264,15 +303,13 @@
     chan_dev = CH // devices
     per_group = AVG // chan_dev
 
+    solutions = jnp.stack([cal_amp * jnp.cos(cal_phase), cal_amp * jnp.sin(cal_phase)])
     my_index = lax.dynamic_slice_in_dim(cal_index, myself * in_dev, in_dev, 0)
-    selection = (my_index[:, None] == jnp.arange(NCAL, dtype=jnp.int32)[None, :]).astype(jnp.float32)
-    gain_re = jnp.dot(selection, cal_amp * jnp.cos(cal_phase), precision=highest).T
-    gain_im = jnp.dot(selection, cal_amp * jnp.sin(cal_phase), precision=highest).T
-
+    my_index = my_index.reshape(st_dev, 2).T
     if chan_dev == AVG and st_dev % HALF == 0:
-        outgoing, powers, crosses = channelise(voltages, fir_taps, gain_re, gain_im)
+        outgoing, powers, crosses = channelise(voltages, fir_taps, my_index, solutions)
     else:
-        outgoing, powers, crosses = channelise_small(voltages, fir_taps, gain_re, gain_im, chan_dev)
+        outgoing, powers, crosses = channelise_small(voltages, fir_taps, my_index, solutions, chan_dev)
     incoming = lax.all_to_all(outgoing, "chan", split_axis=0, concat_axis=0, tiled=True)
 
 
@@ -288,7 +325,7 @@
 
     cross_power = 2.0 * jnp.sum(crosses.reshape(st_dev, GROUPS, AVG), axis=(0, 2))
     joined = jnp.transpose(incoming, (1, 0, 2, 3)).reshape(2, stations, chan_dev * SPEC)
-    image = beam_images(joined, positions)
+    image = beam_images(joined, steering_tables(positions))
 
     tile_pix = PIX // devices
     device_ids = jnp.arange(devices, dtype=jnp.int32)

time: 84 us -> 81.6 us (0.971)
  local copies, waits for them, and re-layouts: 8.72 us -> 18.5 us
  waiting for transfers between devices: 20.9 us -> 11.6 us
  other arithmetic: 6.84 us -> 3.77 us
  Pallas kernels: 23.4 us -> 25.6 us
  matrix products: 2.25 us -> 0.18 us
    unnamed x14 -> x15, local copies, waits for them, and re-layouts: 2.14 us -> 15.1 us
    all_to_all x1, waiting for transfers between devices: 20.9 us -> 11.6 us  [local(): lax.all_to_all(outgoing, 'chan', split_axis=0, concat_axis=0, tiled=True)]
    another operation x6 -> x5, other arithmetic: 3.9 us -> 1.02 us  [the longest x2 0.83 us: local(): jnp.stack([cal_amp * jnp.cos(cal_phase), cal_amp * jnp.sin(cal_phase)])]
    pallas_call x0 -> x1, Pallas kernels: none -> 2.23 us  [steering_tables(): pl.pallas_call(steering_kernel, out_shape=jax.ShapeDtypeStruct((2, PIX, s...]
    transpose x2 -> x0, local copies, waits for them, and re-layouts: 2.09 us -> none  [the longest x1 2.01 us: channelise(): table = jnp.transpose(dft_table(CH), (2, 3, 1, 0)).reshape(2 * CH, 2 * CH)]
    dot_general x2 -> x0, matrix products: 2.07 us -> none  [the longest x1 1.11 us: local(): jnp.dot(selection, cal_amp * jnp.cos(cal_phase), precision=highest)]
    pallas_call x1, Pallas kernels: 12.3 us -> 10.3 us  [beam_images(): pl.pallas_call(image_kernel, out_shape=jax.ShapeDtypeStruct((PIX // 256,...]
    pallas_call x1, Pallas kernels: 11.1 us -> 13 us  [channelise(): pl.pallas_call(channelise_kernel, out_shape=[jax.ShapeDtypeStruct((GROUPS...]
  transfers between devices with their start and end apart: 1 -> 1, of which waited for: 1 -> 1; matrix products, arithmetic and copies ran while one was open for 2% -> 4% of each run, Pallas kernels for 0% -> 3%
where the time goes in v3:
time: 81.6 us; the launch traced here: 81 us
  Pallas kernels  25.6 us (31%)
  local copies, waits for them, and re-layouts  18.5 us (23%)
  blocking collectives  13.2 us (16%)
  waiting for transfers between devices  11.6 us (14%)
  starting transfers between devices  7.39 us (9%)
  other arithmetic  3.77 us (5%)
  between operations  0.82 us (1%)
    unnamed x15, local copies, waits for them, and re-layouts  15.1 us
    all_to_all x1, blocking collectives, local(): lax.all_to_all(last, 'chan', split_axis=0, concat_axis=0, tiled=True)  13.2 us
    pallas_call x1, Pallas kernels, channelise(): pl.pallas_call(channelise_kernel, out_shape=[jax.ShapeDtypeStruct((GROUPS...  13 us
    all_to_all x1, waiting for transfers between devices, local(): lax.all_to_all(outgoing, 'chan', split_axis=0, concat_axis=0, tiled=True)  11.6 us
    pallas_call x1, Pallas kernels, beam_images(): pl.pallas_call(image_kernel, out_shape=jax.ShapeDtypeStruct((PIX // 256,...  10.3 us
    all_to_all x1, starting transfers between devices, local(): lax.all_to_all(outgoing, 'chan', split_axis=0, concat_axis=0, tiled=True)  7.39 us
    pallas_call x1, Pallas kernels, steering_tables(): pl.pallas_call(steering_kernel, out_shape=jax.ShapeDtypeStruct((2, PIX, s...  2.23 us
    cos x1, other arithmetic, steering_tables(): jnp.cos(phases)  1.68 us
  transfers between devices with their start and end apart: 1, of which 1 were waited for; matrix products, arithmetic and copies ran while one was open for 4% of the time, Pallas kernels for 3%

profile of v3, /device:TPU:0, one launch (start us, length us, event | category | flops | bytes accessed | tf_op | source)
XLA Modules:
  0.0 81.0 jit_solution(6556330280319542191)
XLA Ops:
  0.7 0.8 dynamic_slice.3
  1.4 0.1 reshape.94
  1.6 0.8 %multiply_bitcast_fusion.2 = (f32[1,256,16]{1,2,0:T(8,128)S(1)}, f32[1,256,16]{1,2,0:T(8,128)S(1)}) fusion(f32[256,16]{0,1:T(8,128)} %param.12, f32[256,16]{0,1:T(8,128)} %param.13), kind=kLoop, calls=%fused_computation.16 | loop fusion | flops 8192 | bytes 65536 | tf_op jit(solution)/shard_map/stack | solution.py:306
  2.4 0.1 copy.33.solution_ref
  2.6 1.9 %copy-done.2 = bf16[2,64,12032]{2,1,0:T(8,128)(2,1)S(1)} copy-done((bf16[2,64,12032]{2,1,0:T(8,128)(2,1)S(1)}, bf16[2,64,12032]{2,1,0:T(8,128)(2,1)}, u32[]{:S(2)}) %copy-start.2) | copy-done | bytes 3080216
  4.4 1.0 %copy-done.3 = bf16[512,512]{1,0:T(8,128)(2,1)S(1)} copy-done((bf16[512,512]{1,0:T(8,128)(2,1)S(1)}, bf16[512,512]{1,0:T(8,128)(2,1)}, u32[]{:S(2)}) %copy-start.3) | copy-done | bytes 524312
  5.5 0.7 copy-done.4
  6.2 13.0 %channelise.1 = (bf16[16,2,32,512]{3,2,1,0:T(8,128)(2,1)}, f32[2,32,256]{2,1,0:T(8,128)S(1)}, f32[32,256]{1,0:T(8,128)S(1)}) custom-call(bf16[2,64,12032]{2,1,0:T(8,128)(2,1)S(1)} %copy-done.2, bf16[16,256]{1,0:T(8,128)(2,1)S(1)} %copy-done.4, bf16[512,512]{1,0:T(8,128)(2,1)S(1)} %copy-done.3, s32[2,32]{1,0:T(2,128)S(1)} %bitcast.27, ...), custom_call_target="tpu_custom_call" | custom-call | tf_op jit(solution)/shard_map/channelise/pallas_call | solution.py:250
  19.2 7.4 %all-to-all-start = ((bf16[16,2,32,512]{3,2,1,0:T(8,128)(2,1)}), bf16[16,2,32,512]{3,2,1,0:T(8,128)(2,1)S(1)}, u32[]{:S(2)}, u32[]{:S(2)}) async-start(bf16[16,2,32,512]{3,2,1,0:T(8,128)(2,1)} %get-tuple-element.5), calls=%async_computation | async-start | bytes 2097152 | tf_op jit(solution)/shard_map/all_to_all | solution.py:313
  26.6 0.7 copy.35
  27.4 0.1 reduce.2
  27.6 0.1 reduce_sum.44
  27.9 1.7 %fusion.1 = (f32[2,1,64,512]{3,2,1,0:T(8,128)S(1)}, f32[2,1,64,512]{3,2,1,0:T(8,128)S(1)}) fusion(f32[64]{0:T(128)S(1)} %add_multiply_fusion, f32[2,512]{1,0:T(2,128)} %param.11), kind=kLoop, calls=%fused_computation.5 | loop fusion | flops 131072 | bytes 528640 | tf_op jit(solution)/shard_map/cos | solution.py:211
  29.6 2.2 %steering.1.steer_ref = f32[2,4096,512]{2,1,0:T(8,128)S(1)} custom-call(f32[4,64,512]{2,1,0:T(8,128)S(1)} %bitcast.26), custom_call_target="tpu_custom_call" | custom-call | flops 12582912 | bytes 16777216 | tf_op jit(solution)/shard_map/steering/pallas_call | solution.py:213
  31.9 5.7 %copy-done = f32[2,4096,512]{2,1,0:T(8,128)} copy-done((f32[2,4096,512]{2,1,0:T(8,128)}, f32[2,4096,512]{2,1,0:T(8,128)S(1)}, u32[]{:S(2)}) %copy-start) | copy-done | bytes 16777240
  37.6 0.1 select_reduce_fusion
  37.7 0.2 convolution_divide_fusion
  37.9 11.6 %all-to-all-done = bf16[16,2,32,512]{3,2,1,0:T(8,128)(2,1)S(1)} async-done(((bf16[16,2,32,512]{3,2,1,0:T(8,128)(2,1)}), bf16[16,2,32,512]{3,2,1,0:T(8,128)(2,1)S(1)}, u32[]{:S(2)}, u32[]{:S(2)}) %all-to-all-start) | async-done | bytes 1048608 | tf_op jit(solution)/shard_map/all_to_all | solution.py:313
  49.6 5.8 %copy-done.1 = f32[2,4096,512]{2,1,0:T(8,128)S(1)} copy-done((f32[2,4096,512]{2,1,0:T(8,128)S(1)}, f32[2,4096,512]{2,1,0:T(8,128)}, u32[]{:S(2)}) %copy-start.1) | copy-done | bytes 16777240
  55.4 10.3 %beam_images.1 = f32[16,256]{1,0:T(8,128)S(1)} custom-call(bf16[2,512,512]{2,1,0:T(8,128)(2,1)S(1)} %bitcast.25, f32[2,4096,512]{2,1,0:T(8,128)S(1)} %copy-done.1), custom_call_target="tpu_custom_call" | custom-call | tf_op jit(solution)/shard_map/beam_images/pallas_call | solution.py:229
  65.7 0.6 gather_fusion
  66.4 13.2 %all_to_all.17 = f32[16,1,336]{2,1,0:T(1,128)S(1)} all-to-all(f32[16,1,336]{2,1,0:T(1,128)S(1)} %copy.37), channel_id=1, replica_groups=mesh['grp'=2,'chan'=16] {'chan'}, dimensions={0} | all-to-all | bytes 43008 | tf_op jit(solution)/shard_map/all_to_all | solution.py:339
  79.7 0.7 fusion.3
  80.4 0.7 reshape.99
  (30 shorter events, 0.7 us)
Async XLA Ops:
  0.6 37.1 %copy-start.5 = (s32[16]{0:T(128)S(1)}, s32[16]{0:T(128)}, u32[]{:S(2)}) copy-start(s32[16]{0:T(128)} %param.15) | copy-start | bytes 196
  0.6 36.9 %copy-start.6 = (s32[16]{0:T(128)S(1)}, s32[16]{0:T(128)}, u32[]{:S(2)}) copy-start(s32[16]{0:T(128)} %param.16) | copy-start | bytes 196
  2.6 1.9 %copy-start.2 = (bf16[2,64,12032]{2,1,0:T(8,128)(2,1)S(1)}, bf16[2,64,12032]{2,1,0:T(8,128)(2,1)}, u32[]{:S(2)}) copy-start(bf16[2,64,12032]{2,1,0:T(8,128)(2,1)} %volt_ref.1) | copy-start | bytes 9240580
  4.4 1.0 %copy-start.3 = (bf16[512,512]{1,0:T(8,128)(2,1)S(1)}, bf16[512,512]{1,0:T(8,128)(2,1)}, u32[]{:S(2)}) copy-start(bf16[512,512]{1,0:T(8,128)(2,1)} %constant.37.clone.table_ref) | copy-start | bytes 1572868
  5.5 0.7 copy-start.4
  19.2 30.3 %all-to-all-start = ((bf16[16,2,32,512]{3,2,1,0:T(8,128)(2,1)}), bf16[16,2,32,512]{3,2,1,0:T(8,128)(2,1)S(1)}, u32[]{:S(2)}, u32[]{:S(2)}) async-start(bf16[16,2,32,512]{3,2,1,0:T(8,128)(2,1)} %get-tuple-element.5), calls=%async_computation | async-start | bytes 2097152 | tf_op jit(solution)/shard_map/all_to_all | solution.py:313
  31.9 5.7 %copy-start = (f32[2,4096,512]{2,1,0:T(8,128)}, f32[2,4096,512]{2,1,0:T(8,128)S(1)}, u32[]{:S(2)}) copy-start(f32[2,4096,512]{2,1,0:T(8,128)S(1)} %steering.1.steer_ref) | copy-start | bytes 50331652
  49.6 5.8 %copy-start.1 = (f32[2,4096,512]{2,1,0:T(8,128)S(1)}, f32[2,4096,512]{2,1,0:T(8,128)}, u32[]{:S(2)}) copy-start(f32[2,4096,512]{2,1,0:T(8,128)} %copy-done) | copy-start | bytes 50331652

commit v4 on v3

--- a/solution.py
+++ b/solution.py
@@ -60,24 +60,23 @@
     fir = fir_ref[...].astype(jnp.float32)
     for t in range(TAPS):
         taps_ref[t] = jnp.broadcast_to(fir[t : t + 1], (8, length))
-    group_ids = lax.broadcasted_iota(jnp.int32, (GROUPS, length), 0)
-    spread = (
-        group_ids == lax.broadcasted_iota(jnp.int32, (GROUPS, length), 1) // AVG
+    chosen = (
+        lax.broadcasted_iota(jnp.int32, (NCAL, in_dev), 0) == index_ref[...]
     ).astype(jnp.float32)
-    solution_ids = lax.broadcasted_iota(jnp.int32, (NCAL, st_dev), 0)
-    for pol in range(2):
-        chosen = (solution_ids == index_ref[pol : pol + 1, :]).astype(jnp.float32)
-        for q in range(2):
-            picked = lax.dot_general(
-                chosen,
-                solution_ref[q],
-                (((0,), (0,)), ((), ())),
-                precision=highest,
-                preferred_element_type=jnp.float32,
-            )
-            gain_ref[pol * 2 + q] = jnp.dot(
-                picked, spread, precision=highest, preferred_element_type=jnp.float32
-            )
+    picked = lax.dot_general(
+        chosen,
+        solution_ref[...],
+        (((0,), (0,)), ((), ())),
+        precision=highest,
+        preferred_element_type=jnp.float32,
+    )
+    column_ids = lax.broadcasted_iota(jnp.int32, (2 * GROUPS, length), 0)
+    group_ids = lax.broadcasted_iota(jnp.int32, (2 * GROUPS, length), 1) // AVG
+    for q in range(2):
+        spread = (column_ids == group_ids + q * GROUPS).astype(jnp.float32)
+        gains = jnp.dot(picked, spread, precision=highest, preferred_element_type=jnp.float32)
+        gain_ref[q] = gains[:st_dev]
+        gain_ref[2 + q] = gains[st_dev:]
 
     @pl.loop(0, SPEC // STEP)
     def _(block):
@@ -178,11 +177,19 @@
         odd_ref[rows, :] = jnp.where(same, 0.0, -2.0 * odd).astype(jnp.bfloat16)
 
     tile = out_ref.shape[1]
-
-    @pl.loop(0, out_ref.shape[0], unroll=2)
+    lines = tile // SIDE
+
+    @pl.loop(0, out_ref.shape[0], unroll=4)
     def _(block):
-        pixels = pl.ds(pl.multiple_of(block * tile, tile), tile)
-        cosine, sine = steer_ref[0, pixels, :], steer_ref[1, pixels, :]
+        cosines, sines = [], []
+        for line in range(lines):
+            u = block * lines + line
+            east_cos = steer_ref[0, pl.ds(u, 1), :]
+            east_sin = steer_ref[1, pl.ds(u, 1), :]
+            cosines.append(east_cos * steer_ref[2] - east_sin * steer_ref[3])
+            sines.append(east_sin * steer_ref[2] + east_cos * steer_ref[3])
+        cosine = jnp.concatenate(cosines, axis=0)
+        sine = jnp.concatenate(sines, axis=0)
         cos16, sin16 = cosine.astype(jnp.bfloat16), sine.astype(jnp.bfloat16)
         first = jnp.dot(cos16, even_ref[...], preferred_element_type=jnp.float32)
         first = first + jnp.dot(sin16, odd_ref[...], preferred_element_type=jnp.float32)
@@ -194,33 +201,73 @@
         out_ref[pl.ds(block, 1), :] = jnp.sum(folded.T, axis=0, keepdims=True)
 
 
-def steering_kernel(axis_ref, out_ref):
-    @pl.loop(0, SIDE)
-    def _(u):
-        east_cos = axis_ref[0, pl.ds(u, 1), :]
-        east_sin = axis_ref[1, pl.ds(u, 1), :]
-        pixels = pl.ds(pl.multiple_of(u * SIDE, SIDE), SIDE)
-        out_ref[0, pixels, :] = east_cos * axis_ref[2] - east_sin * axis_ref[3]
-        out_ref[1, pixels, :] = east_sin * axis_ref[2] + east_cos * axis_ref[3]
-
-
-def steering_tables(positions):
+def exchange_kernel(source_ref, target_ref, sent, landed, own):
+    count = source_ref.shape[0]
+    me = lax.axis_index("chan")
+    barrier = pltpu.get_barrier_semaphore()
+
+    @pl.loop(1, count)
+    def _(step):
+        pl.semaphore_signal(
+            barrier,
+            inc=1,
+            device_id={"chan": lax.rem(me + step, count)},
+            device_id_type=pl.DeviceIdType.MESH,
+        )
+
+    local_copy = pltpu.make_async_copy(source_ref.at[me], target_ref.at[me], own)
+    local_copy.start()
+    pl.semaphore_wait(barrier, count - 1)
+
+    def transfer(step, slot):
+        peer = lax.rem(me + step, count)
+        return pltpu.make_async_remote_copy(
+            src_ref=source_ref.at[peer],
+            dst_ref=target_ref.at[slot],
+            send_sem=sent.at[step],
+            recv_sem=landed.at[step],
+            device_id={"chan": peer},
+            device_id_type=pl.DeviceIdType.MESH,
+        )
+
+    @pl.loop(1, count)
+    def _(step):
+        transfer(step, me).start()
+
+    local_copy.wait()
+
+    @pl.loop(1, count)
+    def _(step):
+        transfer(step, lax.rem(me + count - step, count)).wait()
+
+
+def exchange(blocks, number):
+    count = blocks.shape[0]
+    if count > 16:
+        return lax.all_to_all(blocks, "chan", split_axis=0, concat_axis=0, tiled=True)
+    vmem = pl.BlockSpec(memory_space=pltpu.VMEM)
+    return pl.pallas_call(
+        exchange_kernel,
+        out_shape=jax.ShapeDtypeStruct(blocks.shape, blocks.dtype),
+        in_specs=[vmem],
+        out_specs=vmem,
+        scratch_shapes=[
+            pltpu.SemaphoreType.DMA((count,)),
+            pltpu.SemaphoreType.DMA((count,)),
+            pltpu.SemaphoreType.DMA,
+        ],
+        compiler_params=pltpu.CompilerParams(
+            collective_id=number, has_side_effects=True, vmem_limit_bytes=16 * 1024 * 1024
+        ),
+        name="exchange",
+    )(blocks)
+
+
+def steering_axes(positions):
     steps = (jnp.arange(SIDE, dtype=jnp.float32) - SIDE // 2) / jnp.float32(SIDE)
     phases = jnp.float32(2.0 * math.pi) * (positions[:, None, :] * steps[None, :, None])
     stations = positions.shape[1]
-    axes = jnp.stack([jnp.cos(phases), jnp.sin(phases)], axis=1).reshape(4, SIDE, stations)
-    vmem = pl.BlockSpec(memory_space=pltpu.VMEM)
-    return pl.pallas_call(
-        steering_kernel,
-        out_shape=jax.ShapeDtypeStruct((2, PIX, stations), jnp.float32),
-        in_specs=[vmem],
-        out_specs=vmem,
-        cost_estimate=pl.CostEstimate(
-            flops=6 * PIX * stations, bytes_accessed=8 * PIX * stations, transcendentals=0
-        ),
-        compiler_params=pltpu.CompilerParams(vmem_limit_bytes=24 * 1024 * 1024),
-        name="steering",
-    )(axes)
+    return jnp.stack([jnp.cos(phases), jnp.sin(phases)], axis=1).reshape(4, SIDE, stations)
 
 
 def beam_images(joined, steer):
@@ -307,10 +354,15 @@
     my_index = lax.dynamic_slice_in_dim(cal_index, myself * in_dev, in_dev, 0)
     my_index = my_index.reshape(st_dev, 2).T
     if chan_dev == AVG and st_dev % HALF == 0:
-        outgoing, powers, crosses = channelise(voltages, fir_taps, my_index, solutions)
+        outgoing, powers, crosses = channelise(
+            voltages,
+            fir_taps,
+            my_index.reshape(1, in_dev),
+            jnp.concatenate([solutions[0], solutions[1]], axis=1),
+        )
     else:
         outgoing, powers, crosses = channelise_small(voltages, fir_taps, my_index, solutions, chan_dev)
-    incoming = lax.all_to_all(outgoing, "chan", split_axis=0, concat_axis=0, tiled=True)
+    incoming = exchange(outgoing, 0)
 
 
     power_rows = jnp.transpose(powers, (2, 1, 0)).reshape(CH, in_dev) / jnp.float32(SPEC)
@@ -325,7 +377,7 @@
 
     cross_power = 2.0 * jnp.sum(crosses.reshape(st_dev, GROUPS, AVG), axis=(0, 2))
     joined = jnp.transpose(incoming, (1, 0, 2, 3)).reshape(2, stations, chan_dev * SPEC)
-    image = beam_images(joined, steering_tables(positions))
+    image = beam_images(joined, steering_axes(positions))
 
     tile_pix = PIX // devices
     device_ids = jnp.arange(devices, dtype=jnp.int32)
@@ -336,7 +388,9 @@
     last = jnp.concatenate(
         [tiles, sub_rows, jnp.broadcast_to(cross_power[None], (devices, GROUPS))], axis=1
     )
-    arrived = lax.all_to_all(last, "chan", split_axis=0, concat_axis=0, tiled=True)
+    width = last.shape[1]
+    padded = jnp.pad(last, ((0, 0), (0, 8 * LANES - width))).reshape(devices, 8, LANES)
+    arrived = exchange(padded, 1).reshape(devices, 8 * LANES)[:, :width]
     scale = jnp.float32(1.0 / (SPEC * AVG) * math.sqrt(SPEC * AVG) / (2 * stations))
     pieces = jnp.sum(arrived[:, :tile_pix].reshape(GROUPS, per_group, tile_pix), axis=1)
     constant = jnp.sum(arrived[:, tile_pix + in_dev :], axis=0)

time: 81.6 us -> 68.4 us (0.84)
  Pallas kernels: 25.6 us -> 57.4 us
  blocking collectives: 13.2 us -> 0 us
  local copies, waits for them, and re-layouts: 18.5 us -> 6.46 us
  waiting for transfers between devices: 11.6 us -> 0 us
  starting transfers between devices: 7.39 us -> 0 us
    pallas_call x1 -> x2, Pallas kernels: 2.23 us -> 36.1 us  [exchange(): pl.pallas_call(exchange_kernel, out_shape=jax.ShapeDtypeStruct(blocks.sha...]
    all_to_all x1 -> x0, blocking collectives: 13.2 us -> none  [local(): lax.all_to_all(last, 'chan', split_axis=0, concat_axis=0, tiled=True)]
    all_to_all x1 -> x0, waiting for transfers between devices: 11.6 us -> none  [local(): lax.all_to_all(outgoing, 'chan', split_axis=0, concat_axis=0, tiled=True)]
    unnamed x15, local copies, waits for them, and re-layouts: 15.1 us -> 3.66 us
    all_to_all x1 -> x0, starting transfers between devices: 7.39 us -> none  [local(): lax.all_to_all(outgoing, 'chan', split_axis=0, concat_axis=0, tiled=True)]
    pallas_call x1, Pallas kernels: 13 us -> 11.5 us  [channelise(): pl.pallas_call(channelise_kernel, out_shape=[jax.ShapeDtypeStruct((GROUPS...]
    another operation x5 -> x3, other arithmetic: 1.02 us -> 0.19 us  [the longest x2 0.83 us: local(): jnp.stack([cal_amp * jnp.cos(cal_phase), cal_amp * jnp.sin(cal_phase)])]
    mul x0 -> x1, other arithmetic: none -> 0.82 us  [local(): cal_amp * jnp.cos(cal_phase)]
  transfers between devices with their start and end apart: 1 -> 0, of which waited for: 1 -> 0; matrix products, arithmetic and copies ran while one was open for 4% -> 0% of each run, Pallas kernels for 3% -> 0%
where the time goes in v4:
time: 68.4 us; the launch traced here: 68 us
  Pallas kernels  57.4 us (84%)
  local copies, waits for them, and re-layouts  6.46 us (9%)
  other arithmetic  3.09 us (5%)
  between operations  0.83 us (1%)
    pallas_call x2, Pallas kernels, exchange(): pl.pallas_call(exchange_kernel, out_shape=jax.ShapeDtypeStruct(blocks.sha...  36.1 us
    pallas_call x1, Pallas kernels, channelise(): pl.pallas_call(channelise_kernel, out_shape=[jax.ShapeDtypeStruct((GROUPS...  11.5 us
    pallas_call x1, Pallas kernels, beam_images(): pl.pallas_call(image_kernel, out_shape=jax.ShapeDtypeStruct((PIX // 256,...  9.81 us
    unnamed x15, local copies, waits for them, and re-layouts  3.66 us

profile of v4, /device:TPU:0, one launch (start us, length us, event | category | flops | bytes accessed | tf_op | source)
XLA Modules:
  0.0 68.0 jit_solution(15187484475710873208)
XLA Ops:
  0.6 0.8 %dynamic_slice.3 = s32[64]{0:T(128)S(1)} dynamic-slice(s32[1024]{0:T(1024)} %param.14, s32[]{:T(128)S(6)} %select_n.17), dynamic_slice_sizes={64} | dynamic-slice | bytes 516 | tf_op jit(solution)/shard_map/dynamic_slice | solution.py:354
  1.4 0.1 reshape.101
  1.6 0.1 reshape.102.index_ref
  1.7 0.8 %cosine_multiply_fusion = (f32[256,16]{0,1:T(8,128)S(1)}, f32[256,16]{0,1:T(8,128)S(1)}) fusion(f32[256,16]{0,1:T(8,128)} %param.12, f32[256,16]{0,1:T(8,128)} %param.13), kind=kLoop, calls=%fused_computation.17 | loop fusion | flops 8192 | bytes 65536 | tf_op jit(solution)/shard_map/mul | solution.py:353
  2.5 0.1 copy.32.solution_ref
  2.6 1.9 %copy-done = bf16[2,64,12032]{2,1,0:T(8,128)(2,1)S(1)} copy-done((bf16[2,64,12032]{2,1,0:T(8,128)(2,1)S(1)}, bf16[2,64,12032]{2,1,0:T(8,128)(2,1)}, u32[]{:S(2)}) %copy-start) | copy-done | bytes 3080216
  4.5 1.0 %copy-done.1 = bf16[512,512]{1,0:T(8,128)(2,1)S(1)} copy-done((bf16[512,512]{1,0:T(8,128)(2,1)S(1)}, bf16[512,512]{1,0:T(8,128)(2,1)}, u32[]{:S(2)}) %copy-start.1) | copy-done | bytes 524312
  5.5 0.7 %copy-done.2 = bf16[16,256]{1,0:T(8,128)(2,1)S(1)} copy-done((bf16[16,256]{1,0:T(8,128)(2,1)S(1)}, bf16[16,256]{1,0:T(8,128)(2,1)}, u32[]{:S(2)}) %copy-start.2) | copy-done | bytes 8216
  6.2 11.5 %channelise.1 = (bf16[16,2,32,512]{3,2,1,0:T(8,128)(2,1)S(1)}, f32[2,32,256]{2,1,0:T(8,128)S(1)}, f32[32,256]{1,0:T(8,128)S(1)}) custom-call(bf16[2,64,12032]{2,1,0:T(8,128)(2,1)S(1)} %copy-done, bf16[16,256]{1,0:T(8,128)(2,1)S(1)} %copy-done.2, bf16[512,512]{1,0:T(8,128)(2,1)S(1)} %copy-done.1, s32[1,64]{1,0:T(1,128)S(1)} %reshape.102.index_ref, ...), custom_call_target="tpu_custom_call" | custom-call | tf_op jit(solution)/shard_map/channelise/pallas_call | solution.py:297
  17.9 0.1 copy.34
  18.0 0.1 reduce.2
  18.1 0.2 convolution_divide_fusion
  18.3 23.8 %exchange.2 = bf16[16,2,32,512]{3,2,1,0:T(8,128)(2,1)S(1)} custom-call(bf16[16,2,32,512]{3,2,1,0:T(8,128)(2,1)S(1)} %get-tuple-element.5.source_ref), custom_call_target="tpu_custom_call" | custom-call | tf_op jit(solution)/shard_map/exchange/pallas_call | solution.py:249
  42.1 0.1 copy.33
  42.2 1.0 %fusion.1 = (f32[2,1,64,512]{3,2,1,0:T(8,128)S(1)}, f32[2,1,64,512]{3,2,1,0:T(8,128)S(1)}) fusion(f32[64]{0:T(128)S(1)} %add_multiply_fusion, f32[2,512]{1,0:T(2,128)S(1)} %copy-done.3), kind=kLoop, calls=%fused_computation.5 | loop fusion | flops 131072 | bytes 528640 | tf_op jit(solution)/shard_map/cos | solution.py:270
  43.3 9.8 %beam_images.1 = f32[16,256]{1,0:T(8,128)S(1)} custom-call(bf16[2,512,512]{2,1,0:T(8,128)(2,1)S(1)} %bitcast.23, f32[4,64,512]{2,1,0:T(8,128)S(1)} %bitcast.25), custom_call_target="tpu_custom_call" | custom-call | tf_op jit(solution)/shard_map/beam_images/pallas_call | solution.py:276
  53.1 0.1 select_reduce_fusion
  53.2 0.6 gather_fusion
  53.8 0.1 reduce_sum.43
  53.9 0.1 reduce_sum.44
  54.2 12.4 %exchange.3 = f32[16,8,128]{2,1,0:T(8,128)S(1)} custom-call(f32[16,8,128]{2,1,0:T(8,128)S(1)} %bitcast.26), custom_call_target="tpu_custom_call" | custom-call | tf_op jit(solution)/shard_map/exchange/pallas_call | solution.py:249
  66.6 0.1 slice_reduce_fusion
  66.6 0.7 %fusion.3 = f32[1,16,256]{2,1,0:T(8,128)} fusion(f32[16,1024]{1,0:T(8,128)S(1)} %bitcast.29, f32[16]{0:T(128)S(1)} %slice_reduce_fusion), kind=kLoop, calls=%fused_computation.13 | loop fusion | flops 8192 | bytes 32832 | tf_op jit(solution)/shard_map/mul | solution.py:397
  67.3 0.7 reshape.109
  (28 shorter events, 0.5 us)
Async XLA Ops:
  0.6 17.2 %copy-start.4 = (s32[16]{0:T(128)S(1)}, s32[16]{0:T(128)}, u32[]{:S(2)}) copy-start(s32[16]{0:T(128)} %param.15) | copy-start | bytes 196
  2.6 1.9 %copy-start = (bf16[2,64,12032]{2,1,0:T(8,128)(2,1)S(1)}, bf16[2,64,12032]{2,1,0:T(8,128)(2,1)}, u32[]{:S(2)}) copy-start(bf16[2,64,12032]{2,1,0:T(8,128)(2,1)} %volt_ref.1) | copy-start | bytes 9240580
  4.5 1.0 %copy-start.1 = (bf16[512,512]{1,0:T(8,128)(2,1)S(1)}, bf16[512,512]{1,0:T(8,128)(2,1)}, u32[]{:S(2)}) copy-start(bf16[512,512]{1,0:T(8,128)(2,1)} %constant.38.clone.table_ref) | copy-start | bytes 1572868
  5.5 0.7 %copy-start.2 = (bf16[16,256]{1,0:T(8,128)(2,1)S(1)}, bf16[16,256]{1,0:T(8,128)(2,1)}, u32[]{:S(2)}) copy-start(bf16[16,256]{1,0:T(8,128)(2,1)} %fir_ref.1) | copy-start | bytes 24580
  17.7 24.5 %copy-start.3 = (f32[2,512]{1,0:T(2,128)S(1)}, f32[2,512]{1,0:T(2,128)}, u32[]{:S(2)}) copy-start(f32[2,512]{1,0:T(2,128)} %param.11) | copy-start | bytes 12292
  42.1 11.0 %copy-start.5 = (s32[16]{0:T(128)S(1)}, s32[16]{0:T(128)}, u32[]{:S(2)}) copy-start(s32[16]{0:T(128)} %param.16) | copy-start | bytes 196

commit v5 on v4

--- a/solution.py
+++ b/solution.py
@@ -48,8 +48,38 @@
 
 def channelise_kernel(
     volt_ref, fir_ref, table_ref, index_ref, solution_ref, out_ref, power_ref, cross_ref,
-    filt, spec, taps_ref, gain_ref,
+    filt, spec, taps_ref, gain_ref, stage, sent, landed, own,
 ):
+    count = stage.shape[1]
+    blocks = SPEC // STEP
+    me = lax.axis_index("chan")
+    barrier = pltpu.get_barrier_semaphore()
+
+    @pl.loop(1, count)
+    def _(step):
+        pl.semaphore_signal(
+            barrier,
+            inc=1,
+            device_id={"chan": lax.rem(me + step, count)},
+            device_id_type=pl.DeviceIdType.MESH,
+        )
+
+    pl.semaphore_wait(barrier, count - 1)
+
+    def transfer(block, step, slot):
+        peer = lax.rem(me + step, count)
+        return pltpu.make_async_remote_copy(
+            src_ref=stage.at[block, peer],
+            dst_ref=out_ref.at[block, slot],
+            send_sem=sent.at[block, step],
+            recv_sem=landed.at[block, step],
+            device_id={"chan": peer},
+            device_id_type=pl.DeviceIdType.MESH,
+        )
+
+    def keep_own(block):
+        return pltpu.make_async_copy(stage.at[block, me], out_ref.at[block, me], own.at[block])
+
     length = fir_ref.shape[1]
     in_dev = volt_ref.shape[1]
     st_dev = in_dev // 2
@@ -152,9 +182,22 @@
                             planes[s] = jnp.where(keep, low, pltpu.roll(high, shift, 1))
                             planes[s + bit] = jnp.where(keep, pltpu.roll(low, LANES - shift, 1), high)
                         bit *= 2
-                    where = pl.ds(pl.multiple_of(block * LANES, LANES), LANES)
                     for d in range(STEP):
-                        out_ref[j * STEP + d, q, st_rows, where] = planes[d].astype(jnp.bfloat16)
+                        stage[block, j * STEP + d, q, st_rows, :] = planes[d].astype(jnp.bfloat16)
+
+        keep_own(block).start()
+
+        @pl.loop(1, count)
+        def _(step):
+            transfer(block, step, me).start()
+
+    @pl.loop(0, blocks)
+    def _(block):
+        keep_own(block).wait()
+
+        @pl.loop(1, count)
+        def _(step):
+            transfer(block, step, lax.rem(me + count - step, count)).wait()
 
 
 def image_kernel(data_ref, steer_ref, out_ref, even_ref, odd_ref, along, turned):
@@ -297,7 +340,7 @@
     return pl.pallas_call(
         channelise_kernel,
         out_shape=[
-            jax.ShapeDtypeStruct((GROUPS, 2, st_dev, AVG * SPEC), jnp.bfloat16),
+            jax.ShapeDtypeStruct((SPEC // STEP, GROUPS, 2, st_dev, LANES), jnp.bfloat16),
             jax.ShapeDtypeStruct((2, st_dev, CH), jnp.float32),
             jax.ShapeDtypeStruct((st_dev, CH), jnp.float32),
         ],
@@ -308,8 +351,14 @@
             pltpu.VMEM((2 * CH // LANES, STEP * in_dev, LANES), jnp.float32),
             pltpu.VMEM((TAPS, 8, CH), jnp.float32),
             pltpu.VMEM((4, st_dev, CH), jnp.float32),
+            pltpu.VMEM((SPEC // STEP, GROUPS, 2, st_dev, LANES), jnp.bfloat16),
+            pltpu.SemaphoreType.DMA((SPEC // STEP, GROUPS)),
+            pltpu.SemaphoreType.DMA((SPEC // STEP, GROUPS)),
+            pltpu.SemaphoreType.DMA((SPEC // STEP,)),
         ],
-        compiler_params=pltpu.CompilerParams(vmem_limit_bytes=32 * 1024 * 1024),
+        compiler_params=pltpu.CompilerParams(
+            collective_id=0, has_side_effects=True, vmem_limit_bytes=32 * 1024 * 1024
+        ),
         name="channelise",
     )(voltages, fir_taps, table, my_index, solutions)
 
@@ -354,7 +403,7 @@
     my_index = lax.dynamic_slice_in_dim(cal_index, myself * in_dev, in_dev, 0)
     my_index = my_index.reshape(st_dev, 2).T
     if chan_dev == AVG and st_dev % HALF == 0:
-        outgoing, powers, crosses = channelise(
+        incoming, powers, crosses = channelise(
             voltages,
             fir_taps,
             my_index.reshape(1, in_dev),
@@ -362,7 +411,7 @@
         )
     else:
         outgoing, powers, crosses = channelise_small(voltages, fir_taps, my_index, solutions, chan_dev)
-    incoming = exchange(outgoing, 0)
+        incoming = exchange(outgoing, 0)[None]
 
 
     power_rows = jnp.transpose(powers, (2, 1, 0)).reshape(CH, in_dev) / jnp.float32(SPEC)
@@ -376,7 +425,7 @@
     sub_rows = jnp.dot(member, power_rows, precision=highest) / divisor[:, None]
 
     cross_power = 2.0 * jnp.sum(crosses.reshape(st_dev, GROUPS, AVG), axis=(0, 2))
-    joined = jnp.transpose(incoming, (1, 0, 2, 3)).reshape(2, stations, chan_dev * SPEC)
+    joined = jnp.transpose(incoming, (2, 1, 3, 0, 4)).reshape(2, stations, chan_dev * SPEC)
     image = beam_images(joined, steering_axes(positions))
 
     tile_pix = PIX // devices

time: 68.4 us -> 62.6 us (0.915)
  Pallas kernels: 57.4 us -> 50.4 us
  local copies, waits for them, and re-layouts: 6.46 us -> 7.65 us
    pallas_call x2 -> x1, Pallas kernels: 36.1 us -> 8.4 us  [exchange(): pl.pallas_call(exchange_kernel, out_shape=jax.ShapeDtypeStruct(blocks.sha...]
    pallas_call x1, Pallas kernels: 11.5 us -> 32.2 us  [channelise(): pl.pallas_call(channelise_kernel, out_shape=[jax.ShapeDtypeStruct((SPEC /...]
    transpose x1, local copies, waits for them, and re-layouts: 0.1 us -> 0.84 us  [local(): jnp.transpose(incoming, (2, 1, 3, 0, 4))]
where the time goes in v5:
time: 62.6 us; the launch traced here: 62.1 us
  Pallas kernels  50.4 us (81%)
  local copies, waits for them, and re-layouts  7.65 us (12%)
  other arithmetic  3.09 us (5%)
  between operations  0.83 us (1%)
    pallas_call x1, Pallas kernels, channelise(): pl.pallas_call(channelise_kernel, out_shape=[jax.ShapeDtypeStruct((SPEC /...  32.2 us
    pallas_call x1, Pallas kernels, beam_images(): pl.pallas_call(image_kernel, out_shape=jax.ShapeDtypeStruct((PIX // 256,...  9.81 us
    pallas_call x1, Pallas kernels, exchange(): pl.pallas_call(exchange_kernel, out_shape=jax.ShapeDtypeStruct(blocks.sha...  8.4 us
    unnamed x15, local copies, waits for them, and re-layouts  3.66 us

profile of v5, /device:TPU:0, one launch (start us, length us, event | category | flops | bytes accessed | tf_op | source)
XLA Modules:
  0.0 62.1 jit_solution(7540341936512331670)
XLA Ops:
  0.6 0.8 %dynamic_slice.3 = s32[64]{0:T(128)S(1)} dynamic-slice(s32[1024]{0:T(1024)} %param.14, s32[]{:T(128)S(6)} %select_n.17), dynamic_slice_sizes={64} | dynamic-slice | bytes 516 | tf_op jit(solution)/shard_map/dynamic_slice | solution.py:403
  1.4 0.1 reshape.101
  1.6 0.1 reshape.102.index_ref
  1.7 0.8 %cosine_multiply_fusion = (f32[256,16]{0,1:T(8,128)S(1)}, f32[256,16]{0,1:T(8,128)S(1)}) fusion(f32[256,16]{0,1:T(8,128)} %param.12, f32[256,16]{0,1:T(8,128)} %param.13), kind=kLoop, calls=%fused_computation.17 | loop fusion | flops 8192 | bytes 65536 | tf_op jit(solution)/shard_map/mul | solution.py:402
  2.5 0.1 copy.32.solution_ref
  2.6 1.9 %copy-done = bf16[2,64,12032]{2,1,0:T(8,128)(2,1)S(1)} copy-done((bf16[2,64,12032]{2,1,0:T(8,128)(2,1)S(1)}, bf16[2,64,12032]{2,1,0:T(8,128)(2,1)}, u32[]{:S(2)}) %copy-start) | copy-done | bytes 3080216
  4.5 1.0 %copy-done.1 = bf16[512,512]{1,0:T(8,128)(2,1)S(1)} copy-done((bf16[512,512]{1,0:T(8,128)(2,1)S(1)}, bf16[512,512]{1,0:T(8,128)(2,1)}, u32[]{:S(2)}) %copy-start.1) | copy-done | bytes 524312
  5.5 0.7 %copy-done.2 = bf16[16,256]{1,0:T(8,128)(2,1)S(1)} copy-done((bf16[16,256]{1,0:T(8,128)(2,1)S(1)}, bf16[16,256]{1,0:T(8,128)(2,1)}, u32[]{:S(2)}) %copy-start.2) | copy-done | bytes 8216
  6.2 32.2 %channelise.1 = (bf16[4,16,2,32,128]{4,3,2,1,0:T(8,128)(2,1)S(1)}, f32[2,32,256]{2,1,0:T(8,128)S(1)}, f32[32,256]{1,0:T(8,128)S(1)}) custom-call(bf16[2,64,12032]{2,1,0:T(8,128)(2,1)S(1)} %copy-done, bf16[16,256]{1,0:T(8,128)(2,1)S(1)} %copy-done.2, bf16[512,512]{1,0:T(8,128)(2,1)S(1)} %copy-done.1, s32[1,64]{1,0:T(1,128)S(1)} %reshape.102.index_ref, ...), custom_call_target="tpu_custom_call" | custom-call | tf_op jit(solution)/shard_map/channelise/pallas_call | solution.py:340
  38.6 0.1 copy.34
  38.7 0.1 reduce.2
  38.8 0.2 convolution_divide_fusion
  39.0 0.8 %copy.33 = bf16[2,16,32,4,128]{4,3,2,1,0:T(4,128)(2,1)S(1)} copy(bf16[2,16,32,4,128]{4,2,0,1,3:T(8,128)(2,1)S(1)} %bitcast.23) | data formatting | bytes 2097152 | tf_op jit(solution)/shard_map/transpose | solution.py:428
  39.9 0.4 reshape.103.data_ref
  40.3 1.0 %fusion.1 = (f32[2,1,64,512]{3,2,1,0:T(8,128)S(1)}, f32[2,1,64,512]{3,2,1,0:T(8,128)S(1)}) fusion(f32[64]{0:T(128)S(1)} %add_multiply_fusion, f32[2,512]{1,0:T(2,128)S(1)} %copy-done.3), kind=kLoop, calls=%fused_computation.5 | loop fusion | flops 131072 | bytes 528640 | tf_op jit(solution)/shard_map/cos | solution.py:313
  41.4 9.8 %beam_images.1 = f32[16,256]{1,0:T(8,128)S(1)} custom-call(bf16[2,512,512]{2,1,0:T(8,128)(2,1)S(1)} %reshape.103.data_ref, f32[4,64,512]{2,1,0:T(8,128)S(1)} %bitcast.22), custom_call_target="tpu_custom_call" | custom-call | tf_op jit(solution)/shard_map/beam_images/pallas_call | solution.py:319
  51.2 0.1 select_reduce_fusion
  51.3 0.6 gather_fusion
  51.9 0.1 reduce_sum.43
  52.0 0.1 reduce_sum.44
  52.3 8.4 %exchange.1 = f32[16,8,128]{2,1,0:T(8,128)S(1)} custom-call(f32[16,8,128]{2,1,0:T(8,128)S(1)} %bitcast.24), custom_call_target="tpu_custom_call" | custom-call | tf_op jit(solution)/shard_map/exchange/pallas_call | solution.py:292
  60.7 0.1 slice_reduce_fusion
  60.8 0.7 %fusion.3 = f32[1,16,256]{2,1,0:T(8,128)} fusion(f32[16,1024]{1,0:T(8,128)S(1)} %bitcast.27, f32[16]{0:T(128)S(1)} %slice_reduce_fusion), kind=kLoop, calls=%fused_computation.13 | loop fusion | flops 8192 | bytes 32832 | tf_op jit(solution)/shard_map/mul | solution.py:446
  61.5 0.7 %reshape.109 = f32[1,1024]{1,0:T(1,128)} reshape(f32[16,64]{1,0:T(8,128)S(1)} %slice.20) | data formatting | bytes 8192 | tf_op jit(solution)/shard_map/reshape | solution.py:447
  (28 shorter events, 0.5 us)
Async XLA Ops:
  0.6 37.9 %copy-start.4 = (s32[16]{0:T(128)S(1)}, s32[16]{0:T(128)}, u32[]{:S(2)}) copy-start(s32[16]{0:T(128)} %param.15) | copy-start | bytes 196
  2.6 1.9 %copy-start = (bf16[2,64,12032]{2,1,0:T(8,128)(2,1)S(1)}, bf16[2,64,12032]{2,1,0:T(8,128)(2,1)}, u32[]{:S(2)}) copy-start(bf16[2,64,12032]{2,1,0:T(8,128)(2,1)} %volt_ref.1) | copy-start | bytes 9240580
  4.5 1.0 %copy-start.1 = (bf16[512,512]{1,0:T(8,128)(2,1)S(1)}, bf16[512,512]{1,0:T(8,128)(2,1)}, u32[]{:S(2)}) copy-start(bf16[512,512]{1,0:T(8,128)(2,1)} %constant.38.clone.table_ref) | copy-start | bytes 1572868
  5.5 0.7 %copy-start.2 = (bf16[16,256]{1,0:T(8,128)(2,1)S(1)}, bf16[16,256]{1,0:T(8,128)(2,1)}, u32[]{:S(2)}) copy-start(bf16[16,256]{1,0:T(8,128)(2,1)} %fir_ref.1) | copy-start | bytes 24580
  38.4 1.9 %copy-start.3 = (f32[2,512]{1,0:T(2,128)S(1)}, f32[2,512]{1,0:T(2,128)}, u32[]{:S(2)}) copy-start(f32[2,512]{1,0:T(2,128)} %param.11) | copy-start | bytes 12292
  39.8 11.3 %copy-start.5 = (s32[16]{0:T(128)S(1)}, s32[16]{0:T(128)}, u32[]{:S(2)}) copy-start(s32[16]{0:T(128)} %param.16) | copy-start | bytes 196
